TPU v7x, 128 devices: a whole 4x4x4 slice. The times are simulated.
128 devices in a mesh: cx: 8 (over y, core), cy: 16 (over z, x).
Axes of the slice: x: 4, y: 4, z: 4, core: 2. Of those that a mesh axis runs over, the one named last changes fastest.
Arguments:
- params: float32 [14, 2097152], P(None, ('cx', 'cy')), may hold values from -7 to 140, as said below
- requests: int32 [128, 128, 1], P(('cx', 'cy')), may hold values from 0 to 127, as said below
- lists: int32 [8192, 256], P(('cx', 'cy')), may hold values from 0 to 16383, as said below
- list_len: int32 [8192], P(('cx', 'cy')), may hold values from 64 to 256, as said below
- offsets: int32 [8192, 2], P(('cx', 'cy')), may hold values from 0 to 119, as said below
- cotangent: float32 [8192, 3, 256], P(('cx', 'cy')), may hold values from -6 to 6
Outputs:
- image: float32 [8192, 3, 256], P(('cx', 'cy'))
- grads: float32 [14, 2097152], P(None, ('cx', 'cy'))
Inputs may be any that keep to these rules, and one draw needn't show every extreme that they name: `params`: row 2 (depth z) lies in [40, 80) and rises along every tile's list; rows 0 and 1 lie in [0, 16 * 120 z / 1100) and [0, 16 * 68 z / 1100); row 6 (quaternion w) lies in [1, 2]. `requests`: for every owner, each of its 128 blocks is requested exactly once over all devices and slots. The 64 lists of one device together hold each entry of its fetched buffer exactly once. `list_len`: some tile of every device has 256 live entries. `offsets`: column 0 lies below 120, column 1 below 68.
All inputs are finite; a program needn't handle non-finite values.
Results may differ from a plain program's by a relative error of at most 0.0003.
Values sent between devices are 32-bit elements; how exact they have to be, the bound alone decides.
A program may use at most 192 MiB of HBM per device.

v0:
```python
import jax
import jax.numpy as jnp
from jax import lax
from jax.sharding import PartitionSpec as P

SIDE = 16
FOCAL = 1100
BLOCK = 128


def project(params):
    focal = jnp.float32(FOCAL)
    xpos, ypos, depth = (params[0], params[1], params[2])
    svar = [jnp.exp(2.0 * params[3 + i]) for i in range(3)]
    qnorm = jnp.sqrt(params[6] ** 2 + params[7] ** 2 + params[8] ** 2 + params[9] ** 2)
    qw, qx, qy, qz = (params[6] / qnorm, params[7] / qnorm, params[8] / qnorm, params[9] / qnorm)
    rot = [
        [1.0 - 2.0 * (qy * qy + qz * qz), 2.0 * (qx * qy - qw * qz), 2.0 * (qx * qz + qw * qy)],
        [2.0 * (qx * qy + qw * qz), 1.0 - 2.0 * (qx * qx + qz * qz), 2.0 * (qy * qz - qw * qx)],
        [2.0 * (qx * qz - qw * qy), 2.0 * (qy * qz + qw * qx), 1.0 - 2.0 * (qx * qx + qy * qy)],
    ]

    def sigma(i, j):
        return (
            rot[i][0] * rot[j][0] * svar[0]
            + rot[i][1] * rot[j][1] * svar[1]
            + rot[i][2] * rot[j][2] * svar[2]
        )

    j_diag = focal / depth
    j_xz = -focal * xpos / (depth * depth)
    j_yz = -focal * ypos / (depth * depth)
    cov_a = (
        j_diag * j_diag * sigma(0, 0)
        + 2.0 * j_diag * j_xz * sigma(0, 2)
        + j_xz * j_xz * sigma(2, 2)
        + 0.3
    )
    cov_b = (
        j_diag * j_diag * sigma(0, 1)
        + j_diag * j_yz * sigma(0, 2)
        + j_xz * j_diag * sigma(1, 2)
        + j_xz * j_yz * sigma(2, 2)
    )
    cov_c = (
        j_diag * j_diag * sigma(1, 1)
        + 2.0 * j_diag * j_yz * sigma(1, 2)
        + j_yz * j_yz * sigma(2, 2)
        + 0.3
    )
    determ = cov_a * cov_c - cov_b * cov_b
    return jnp.stack(
        [
            focal * xpos / depth,
            focal * ypos / depth,
            cov_c / determ,
            -cov_b / determ,
            cov_a / determ,
            jax.nn.sigmoid(params[10]),
            params[11],
            params[12],
            params[13],
        ]
    )


def tile_image(features, live, offset, strict):
    pixel = jnp.arange(SIDE * SIDE, dtype=jnp.int32)
    pos_x = (offset[0] * SIDE + pixel % SIDE).astype(jnp.float32) + 0.5
    pos_y = (offset[1] * SIDE + pixel // SIDE).astype(jnp.float32) + 0.5
    delta_x = pos_x[:, None] - features[0][None, :]
    delta_y = pos_y[:, None] - features[1][None, :]
    power = (
        -0.5 * (features[2] * delta_x * delta_x + features[4] * delta_y * delta_y)
        - features[3] * delta_x * delta_y
    )
    alpha = jnp.minimum(0.99, features[5] * jnp.exp(power)) * live[None, :]
    log_keep = jnp.log1p(-alpha)
    span = strict.shape[0]
    pieces = log_keep.reshape(log_keep.shape[0], log_keep.shape[1] // span, span)
    within = jnp.einsum("pbk,kj->pbj", pieces, strict, precision=lax.Precision.HIGHEST)
    totals = jnp.sum(pieces, axis=2)
    prior = jnp.cumsum(totals, axis=1) - totals
    before = (within + prior[:, :, None]).reshape(log_keep.shape)
    weight = alpha * jnp.exp(before)
    return jnp.einsum("ck,pk->cp", features[6:9], weight, precision=lax.Precision.HIGHEST)


def fetch_blocks(outgoing):
    return lax.all_to_all(outgoing, ("cx", "cy"), split_axis=1, concat_axis=1, tiled=True)


def return_grads(outgoing):
    return lax.all_to_all(outgoing, ("cx", "cy"), split_axis=1, concat_axis=1, tiled=True)


def per_device(params, requests, lists, list_len, offsets, cotangent):
    peers = lax.axis_size(("cx", "cy"))
    slots = requests.shape[2]
    g_dev = params.shape[1]
    blocks = g_dev // BLOCK
    length = lists.shape[1]
    tiles = lists.shape[0]
    asked = lax.all_to_all(requests, ("cx", "cy"), split_axis=1, concat_axis=0, tiled=True).reshape(
        -1
    )
    picked = jnp.take(params.reshape(14, blocks, BLOCK), asked, axis=1).reshape(14, -1)
    kinds = picked.shape[0]
    fetched = fetch_blocks(picked.reshape(kinds, peers, slots * BLOCK)).reshape(kinds, -1)
    feats, local_pull = jax.vjp(project, fetched)
    entry = jnp.arange(length, dtype=jnp.int32)
    lane_index = jnp.arange(BLOCK, dtype=jnp.int32)
    strict = (lane_index[:, None] < lane_index[None, :]).astype(jnp.float32)

    def per_tile(entries, count, offset, cot):
        live = (entry < count).astype(jnp.float32)
        gathered = jnp.take(feats, entries, axis=1)
        img, pull = jax.vjp(lambda f: tile_image(f, live, offset, strict), gathered)
        return (img, pull(cot)[0])

    def per_group(item):
        return jax.vmap(per_tile)(item[0], item[1], item[2], item[3])

    group = 16
    grouped = tuple(
        (
            arr.reshape((tiles // group, group) + arr.shape[1:])
            for arr in (lists, list_len, offsets, cotangent)
        )
    )
    images, tile_grads = lax.map(per_group, grouped)
    images = images.reshape(tiles, 3, -1)
    flat = jnp.moveaxis(tile_grads.reshape(tiles, 9, length), 1, 0).reshape(9, -1)
    gfeat = jnp.zeros((9, feats.shape[1]), jnp.float32).at[:, lists.reshape(-1)].add(flat)
    sending = local_pull(gfeat)[0]
    landed = return_grads(sending.reshape(kinds, peers, slots * BLOCK)).reshape(kinds, -1)
    per_request = landed
    per_request = per_request.reshape(14, peers * slots, BLOCK)
    onehot = (asked[:, None] == jnp.arange(blocks, dtype=jnp.int32)[None, :]).astype(jnp.float32)
    summed = jnp.einsum("krb,rn->knb", per_request, onehot, precision=lax.Precision.HIGHEST)
    return (images, summed.reshape(14, g_dev))


def solution(mesh):
    in_specs = (
        P(None, ("cx", "cy")),
        P(("cx", "cy"), None, None),
        P(("cx", "cy"), None),
        P(("cx", "cy")),
        P(("cx", "cy"), None),
        P(("cx", "cy"), None, None),
    )
    out_specs = (P(("cx", "cy"), None, None), P(None, ("cx", "cy")))
    return jax.shard_map(
        per_device, mesh=mesh, in_specs=in_specs, out_specs=out_specs, check_vma=False
    )
```

profile of v0, /device:TPU:1, one launch (start us, length us, event | category | flops | bytes accessed | tf_op | source)
XLA Modules:
  0.0 572.3 jit_solution(4792681495936717555)
XLA Ops:
  2.0 11.5 %all-to-all-start = ((s32[1,128,1]{2,0,1:T(1,128)}), s32[1,128,1]{2,0,1:T(1,128)S(1)}, u32[]{:S(2)}, u32[]{:S(2)}) async-start(s32[1,128,1]{2,0,1:T(1,128)} %copy.487), calls=%async_computation | async-start | bytes 131072 | tf_op jit(solution)/shard_map/all_to_all | solution.py:104
  16.5 6.7 %all-to-all-done = s32[1,128,1]{2,0,1:T(1,128)S(1)} async-done(((s32[1,128,1]{2,0,1:T(1,128)}), s32[1,128,1]{2,0,1:T(1,128)S(1)}, u32[]{:S(2)}, u32[]{:S(2)}) %all-to-all-start) | async-done | bytes 544 | tf_op jit(solution)/shard_map/all_to_all | solution.py:104
  32.8 18.9 %all-to-all-done.1 = f32[14,128,128]{2,0,1:T(8,128)S(1)} async-done(((f32[14,128,128]{2,0,1:T(8,128)}), f32[14,128,128]{2,0,1:T(8,128)S(1)}, u32[]{:S(2)}, u32[]{:S(2)}) %all-to-all-start.1) | async-done | bytes 917536 | tf_op jit(solution)/shard_map/all_to_all | solution.py:90
  64.6 262.6 %while.16 = (s32[]{:T(128)}, f32[4,16,3,256]{3,1,0,2:T(8,128)S(1)}, f32[4,16,9,256]{3,2,1,0:T(8,128)}, s32[4,16,256]{2,1,0:T(8,128)S(1)}, f32[9,16384]{0,1:T(8,1...) while((s32[]{:T(128)}, f32[4,16,3,256]{3,1,0,2:T(8,128)S(1)}, ...), condition=%wide.region_11.12_spmd.clone.clone, body=%wide.region_0.11_spmd.clone.clone.sunk | while | flops 3455475200 | bytes 112966760 | solution.py:131
  65.3 14.1 %gather_fusion = f32[4096,9]{1,0:T(8,128)S(1)} fusion(f32[9,16384]{0,1:T(8,128)} %get-tuple-element.524, s32[4096]{0:T(1024)S(1)} %broadcast_clamp_fusion.2), kind=kCustom, calls=%fused_computation.clone.clone.1 | custom fusion | bytes 311296 | tf_op jit(solution)/shard_map/while/body/eval_jaxpr/vmap(jit(_take))/gather | solution.py:117
  84.7 8.0 %add_exponential_fusion.2 = f32[16,256,2,128]{1,3,2,0:T(8,128)S(1)} fusion(f32[16,256,2]{1,2,0:T(2,128)S(1)} %sub.1009, f32[16,2,128]{2,1,0:T(2,128)S(1)} %compare_convert_fusion.2, f32[16,2,128]{2,1,0:T(2,128)S(1)} %bitcast.330, f32[16,2,128]{2,1,0:T(2,128)S(1)} %bitcast.332, f32[16,256]{1,0:T(8,128)S(1)} %convert_add_fusion.4, ...), kind=kOutput, calls=%fused_computation.58.clone.1 | convolution fusion | flops 1627422720 | bytes 4374528 | tf_op jit(solution)/shard_map/while/body/eval_jaxpr/vmap(jvp(pbk,kj->pbj))/dot_general | solution.py:81
  92.8 9.7 %bitcast_reduce_fusion.2 = (f32[16,256,2]{1,2,0:T(2,128)S(1)}, f32[16,256,256]{1,2,0:T(8,128)}, f32[16,256,256]{1,2,0:T(8,128)}) fusion(f32[16,256,2,128]{1,3,2,0:T(8,128)S(1)} %add_exponential_fusion.2, f32[16,256]{1,0:T(8,128)S(1)} %fusion.162, f32[16,256]{1,0:T(8,128)S(1)} %get-tuple-element.483, f32[16,256]{1,0:T(8,128)S(1)} %get-tuple-element.484, ...), kind=kOutput, calls=%fused_computation.110.clone.1 | convolution fusion | flops 55566336 | bytes 12894212 | tf_op jit(solution)/shard_map/while/body/eval_jaxpr/vmap(transpose(jvp(ck,pk->cp)))/dot_general | solution.py:86
  102.6 5.8 %convolution_add_fusion.2 = f32[16,256,2,128]{1,3,2,0:T(8,128)S(1)} fusion(f32[16,256,2,128]{1,3,2,0:T(8,128)} %bitcast.313, f32[16,256,2]{1,2,0:T(2,128)S(1)} %bitcast.320), kind=kOutput, calls=%fused_computation.60.clone.1 | convolution fusion | flops 1611694080 | bytes 8421376 | tf_op jit(solution)/shard_map/while/body/eval_jaxpr/vmap(transpose(jvp(pbk,kj->pbj)))/dot_general | solution.py:81
  108.4 5.9 %fusion.163 = (f32[16,256,256]{1,2,0:T(8,128)S(1)}, f32[16,256,256]{1,2,0:T(8,128)S(1)}) fusion(f32[16,256,2,128]{1,3,2,0:T(8,128)S(1)} %convolution_add_fusion.2, f32[16,256,256]{1,2,0:T(8,128)S(1)} %copy-done.2, f32[16,256,2,128]{1,3,2,0:T(8,128)S(1)} %copy-done.1, f32[16,256]{1,0:T(8,128)S(1)} %fusion.162, f32[16,256]{1,0:T(8,128)S(1)} %get-tuple-element.483, ...), kind=kLoop, calls=%fused_computation.52.clone.1 | loop fusion | flops 28311552 | bytes 21118976 | tf_op jit(solution)/shard_map/while/body/eval_jaxpr/vmap(transpose(jvp()))/mul | solution.py:77
  116.4 9.3 %fusion.164 = (f32[16,256]{1,0:T(8,128)S(1)}, f32[16,256]{1,0:T(8,128)S(1)}, f32[16,256]{1,0:T(8,128)S(1)}, f32[16,256]{1,0:T(8,128)S(1)}, f32[16,256]{1,0:T(8,128)S(1)}, /*index=5*/f32[16,256]{1,0:T(8,128)S(1)}) fusion(f32[16,256]{1,0:T(8,128)S(1)} %get-tuple-element.484, f32[16,256]{1,0:T(8,128)S(1)} %convert_add_fusion.4, ...), kind=kLoop, calls=%fused_computation.45.clone.1 | loop fusion | flops 39821312 | bytes 4423680 | tf_op jit(solution)/shard_map/while/body/eval_jaxpr/vmap(transpose(jvp()))/reduce_sum | solution.py:75
  130.8 14.1 %gather_fusion = f32[4096,9]{1,0:T(8,128)S(1)} fusion(f32[9,16384]{0,1:T(8,128)} %get-tuple-element.524, s32[4096]{0:T(1024)S(1)} %broadcast_clamp_fusion.2), kind=kCustom, calls=%fused_computation.clone.clone.1 | custom fusion | bytes 311296 | tf_op jit(solution)/shard_map/while/body/eval_jaxpr/vmap(jit(_take))/gather | solution.py:117
  150.2 8.1 %add_exponential_fusion.2 = f32[16,256,2,128]{1,3,2,0:T(8,128)S(1)} fusion(f32[16,256,2]{1,2,0:T(2,128)S(1)} %sub.1009, f32[16,2,128]{2,1,0:T(2,128)S(1)} %compare_convert_fusion.2, f32[16,2,128]{2,1,0:T(2,128)S(1)} %bitcast.330, f32[16,2,128]{2,1,0:T(2,128)S(1)} %bitcast.332, f32[16,256]{1,0:T(8,128)S(1)} %convert_add_fusion.4, ...), kind=kOutput, calls=%fused_computation.58.clone.1 | convolution fusion | flops 1627422720 | bytes 4374528 | tf_op jit(solution)/shard_map/while/body/eval_jaxpr/vmap(jvp(pbk,kj->pbj))/dot_general | solution.py:81
  158.3 9.7 %bitcast_reduce_fusion.2 = (f32[16,256,2]{1,2,0:T(2,128)S(1)}, f32[16,256,256]{1,2,0:T(8,128)}, f32[16,256,256]{1,2,0:T(8,128)}) fusion(f32[16,256,2,128]{1,3,2,0:T(8,128)S(1)} %add_exponential_fusion.2, f32[16,256]{1,0:T(8,128)S(1)} %fusion.162, f32[16,256]{1,0:T(8,128)S(1)} %get-tuple-element.483, f32[16,256]{1,0:T(8,128)S(1)} %get-tuple-element.484, ...), kind=kOutput, calls=%fused_computation.110.clone.1 | convolution fusion | flops 55566336 | bytes 12894212 | tf_op jit(solution)/shard_map/while/body/eval_jaxpr/vmap(transpose(jvp(ck,pk->cp)))/dot_general | solution.py:86
  168.1 5.8 %convolution_add_fusion.2 = f32[16,256,2,128]{1,3,2,0:T(8,128)S(1)} fusion(f32[16,256,2,128]{1,3,2,0:T(8,128)} %bitcast.313, f32[16,256,2]{1,2,0:T(2,128)S(1)} %bitcast.320), kind=kOutput, calls=%fused_computation.60.clone.1 | convolution fusion | flops 1611694080 | bytes 8421376 | tf_op jit(solution)/shard_map/while/body/eval_jaxpr/vmap(transpose(jvp(pbk,kj->pbj)))/dot_general | solution.py:81
  173.9 5.9 %fusion.163 = (f32[16,256,256]{1,2,0:T(8,128)S(1)}, f32[16,256,256]{1,2,0:T(8,128)S(1)}) fusion(f32[16,256,2,128]{1,3,2,0:T(8,128)S(1)} %convolution_add_fusion.2, f32[16,256,256]{1,2,0:T(8,128)S(1)} %copy-done.2, f32[16,256,2,128]{1,3,2,0:T(8,128)S(1)} %copy-done.1, f32[16,256]{1,0:T(8,128)S(1)} %fusion.162, f32[16,256]{1,0:T(8,128)S(1)} %get-tuple-element.483, ...), kind=kLoop, calls=%fused_computation.52.clone.1 | loop fusion | flops 28311552 | bytes 21118976 | tf_op jit(solution)/shard_map/while/body/eval_jaxpr/vmap(transpose(jvp()))/mul | solution.py:77
  181.9 9.3 %fusion.164 = (f32[16,256]{1,0:T(8,128)S(1)}, f32[16,256]{1,0:T(8,128)S(1)}, f32[16,256]{1,0:T(8,128)S(1)}, f32[16,256]{1,0:T(8,128)S(1)}, f32[16,256]{1,0:T(8,128)S(1)}, /*index=5*/f32[16,256]{1,0:T(8,128)S(1)}) fusion(f32[16,256]{1,0:T(8,128)S(1)} %get-tuple-element.484, f32[16,256]{1,0:T(8,128)S(1)} %convert_add_fusion.4, ...), kind=kLoop, calls=%fused_computation.45.clone.1 | loop fusion | flops 39821312 | bytes 4423680 | tf_op jit(solution)/shard_map/while/body/eval_jaxpr/vmap(transpose(jvp()))/reduce_sum | solution.py:75
  196.3 14.1 %gather_fusion = f32[4096,9]{1,0:T(8,128)S(1)} fusion(f32[9,16384]{0,1:T(8,128)} %get-tuple-element.524, s32[4096]{0:T(1024)S(1)} %broadcast_clamp_fusion.2), kind=kCustom, calls=%fused_computation.clone.clone.1 | custom fusion | bytes 311296 | tf_op jit(solution)/shard_map/while/body/eval_jaxpr/vmap(jit(_take))/gather | solution.py:117
  215.7 8.0 %add_exponential_fusion.2 = f32[16,256,2,128]{1,3,2,0:T(8,128)S(1)} fusion(f32[16,256,2]{1,2,0:T(2,128)S(1)} %sub.1009, f32[16,2,128]{2,1,0:T(2,128)S(1)} %compare_convert_fusion.2, f32[16,2,128]{2,1,0:T(2,128)S(1)} %bitcast.330, f32[16,2,128]{2,1,0:T(2,128)S(1)} %bitcast.332, f32[16,256]{1,0:T(8,128)S(1)} %convert_add_fusion.4, ...), kind=kOutput, calls=%fused_computation.58.clone.1 | convolution fusion | flops 1627422720 | bytes 4374528 | tf_op jit(solution)/shard_map/while/body/eval_jaxpr/vmap(jvp(pbk,kj->pbj))/dot_general | solution.py:81
  223.8 9.7 %bitcast_reduce_fusion.2 = (f32[16,256,2]{1,2,0:T(2,128)S(1)}, f32[16,256,256]{1,2,0:T(8,128)}, f32[16,256,256]{1,2,0:T(8,128)}) fusion(f32[16,256,2,128]{1,3,2,0:T(8,128)S(1)} %add_exponential_fusion.2, f32[16,256]{1,0:T(8,128)S(1)} %fusion.162, f32[16,256]{1,0:T(8,128)S(1)} %get-tuple-element.483, f32[16,256]{1,0:T(8,128)S(1)} %get-tuple-element.484, ...), kind=kOutput, calls=%fused_computation.110.clone.1 | convolution fusion | flops 55566336 | bytes 12894212 | tf_op jit(solution)/shard_map/while/body/eval_jaxpr/vmap(transpose(jvp(ck,pk->cp)))/dot_general | solution.py:86
  233.6 5.8 %convolution_add_fusion.2 = f32[16,256,2,128]{1,3,2,0:T(8,128)S(1)} fusion(f32[16,256,2,128]{1,3,2,0:T(8,128)} %bitcast.313, f32[16,256,2]{1,2,0:T(2,128)S(1)} %bitcast.320), kind=kOutput, calls=%fused_computation.60.clone.1 | convolution fusion | flops 1611694080 | bytes 8421376 | tf_op jit(solution)/shard_map/while/body/eval_jaxpr/vmap(transpose(jvp(pbk,kj->pbj)))/dot_general | solution.py:81
  239.4 5.9 %fusion.163 = (f32[16,256,256]{1,2,0:T(8,128)S(1)}, f32[16,256,256]{1,2,0:T(8,128)S(1)}) fusion(f32[16,256,2,128]{1,3,2,0:T(8,128)S(1)} %convolution_add_fusion.2, f32[16,256,256]{1,2,0:T(8,128)S(1)} %copy-done.2, f32[16,256,2,128]{1,3,2,0:T(8,128)S(1)} %copy-done.1, f32[16,256]{1,0:T(8,128)S(1)} %fusion.162, f32[16,256]{1,0:T(8,128)S(1)} %get-tuple-element.483, ...), kind=kLoop, calls=%fused_computation.52.clone.1 | loop fusion | flops 28311552 | bytes 21118976 | tf_op jit(solution)/shard_map/while/body/eval_jaxpr/vmap(transpose(jvp()))/mul | solution.py:77
  247.4 9.3 %fusion.164 = (f32[16,256]{1,0:T(8,128)S(1)}, f32[16,256]{1,0:T(8,128)S(1)}, f32[16,256]{1,0:T(8,128)S(1)}, f32[16,256]{1,0:T(8,128)S(1)}, f32[16,256]{1,0:T(8,128)S(1)}, /*index=5*/f32[16,256]{1,0:T(8,128)S(1)}) fusion(f32[16,256]{1,0:T(8,128)S(1)} %get-tuple-element.484, f32[16,256]{1,0:T(8,128)S(1)} %convert_add_fusion.4, ...), kind=kLoop, calls=%fused_computation.45.clone.1 | loop fusion | flops 39821312 | bytes 4423680 | tf_op jit(solution)/shard_map/while/body/eval_jaxpr/vmap(transpose(jvp()))/reduce_sum | solution.py:75
  261.8 14.2 %gather_fusion = f32[4096,9]{1,0:T(8,128)S(1)} fusion(f32[9,16384]{0,1:T(8,128)} %get-tuple-element.524, s32[4096]{0:T(1024)S(1)} %broadcast_clamp_fusion.2), kind=kCustom, calls=%fused_computation.clone.clone.1 | custom fusion | bytes 311296 | tf_op jit(solution)/shard_map/while/body/eval_jaxpr/vmap(jit(_take))/gather | solution.py:117
  281.2 8.0 %add_exponential_fusion.2 = f32[16,256,2,128]{1,3,2,0:T(8,128)S(1)} fusion(f32[16,256,2]{1,2,0:T(2,128)S(1)} %sub.1009, f32[16,2,128]{2,1,0:T(2,128)S(1)} %compare_convert_fusion.2, f32[16,2,128]{2,1,0:T(2,128)S(1)} %bitcast.330, f32[16,2,128]{2,1,0:T(2,128)S(1)} %bitcast.332, f32[16,256]{1,0:T(8,128)S(1)} %convert_add_fusion.4, ...), kind=kOutput, calls=%fused_computation.58.clone.1 | convolution fusion | flops 1627422720 | bytes 4374528 | tf_op jit(solution)/shard_map/while/body/eval_jaxpr/vmap(jvp(pbk,kj->pbj))/dot_general | solution.py:81
  289.3 9.7 %bitcast_reduce_fusion.2 = (f32[16,256,2]{1,2,0:T(2,128)S(1)}, f32[16,256,256]{1,2,0:T(8,128)}, f32[16,256,256]{1,2,0:T(8,128)}) fusion(f32[16,256,2,128]{1,3,2,0:T(8,128)S(1)} %add_exponential_fusion.2, f32[16,256]{1,0:T(8,128)S(1)} %fusion.162, f32[16,256]{1,0:T(8,128)S(1)} %get-tuple-element.483, f32[16,256]{1,0:T(8,128)S(1)} %get-tuple-element.484, ...), kind=kOutput, calls=%fused_computation.110.clone.1 | convolution fusion | flops 55566336 | bytes 12894212 | tf_op jit(solution)/shard_map/while/body/eval_jaxpr/vmap(transpose(jvp(ck,pk->cp)))/dot_general | solution.py:86
  299.1 5.8 %convolution_add_fusion.2 = f32[16,256,2,128]{1,3,2,0:T(8,128)S(1)} fusion(f32[16,256,2,128]{1,3,2,0:T(8,128)} %bitcast.313, f32[16,256,2]{1,2,0:T(2,128)S(1)} %bitcast.320), kind=kOutput, calls=%fused_computation.60.clone.1 | convolution fusion | flops 1611694080 | bytes 8421376 | tf_op jit(solution)/shard_map/while/body/eval_jaxpr/vmap(transpose(jvp(pbk,kj->pbj)))/dot_general | solution.py:81
  304.9 5.9 %fusion.163 = (f32[16,256,256]{1,2,0:T(8,128)S(1)}, f32[16,256,256]{1,2,0:T(8,128)S(1)}) fusion(f32[16,256,2,128]{1,3,2,0:T(8,128)S(1)} %convolution_add_fusion.2, f32[16,256,256]{1,2,0:T(8,128)S(1)} %copy-done.2, f32[16,256,2,128]{1,3,2,0:T(8,128)S(1)} %copy-done.1, f32[16,256]{1,0:T(8,128)S(1)} %fusion.162, f32[16,256]{1,0:T(8,128)S(1)} %get-tuple-element.483, ...), kind=kLoop, calls=%fused_computation.52.clone.1 | loop fusion | flops 28311552 | bytes 21118976 | tf_op jit(solution)/shard_map/while/body/eval_jaxpr/vmap(transpose(jvp()))/mul | solution.py:77
  312.9 9.3 %fusion.164 = (f32[16,256]{1,0:T(8,128)S(1)}, f32[16,256]{1,0:T(8,128)S(1)}, f32[16,256]{1,0:T(8,128)S(1)}, f32[16,256]{1,0:T(8,128)S(1)}, f32[16,256]{1,0:T(8,128)S(1)}, /*index=5*/f32[16,256]{1,0:T(8,128)S(1)}) fusion(f32[16,256]{1,0:T(8,128)S(1)} %get-tuple-element.484, f32[16,256]{1,0:T(8,128)S(1)} %convert_add_fusion.4, ...), kind=kLoop, calls=%fused_computation.45.clone.1 | loop fusion | flops 39821312 | bytes 4423680 | tf_op jit(solution)/shard_map/while/body/eval_jaxpr/vmap(transpose(jvp()))/reduce_sum | solution.py:75
  327.3 6.0 %copy.507 = f32[9,64,256]{0,2,1:T(8,128)} copy(f32[9,64,256]{2,0,1:T(8,128)} %bitcast.347) | data formatting | bytes 1179648 | tf_op jit(solution)/shard_map/transpose | solution.py:133
  333.3 91.4 %scatter_custom_fusion = f32[9,16384]{0,1:T(8,128)} fusion(s32[16384]{0:T(1024)S(1)} %bitcast.370, f32[16384,9]{1,0:T(8,128)} %bitcast.315, f32[]{:T(128)} %constant.151.clone.1), kind=kCustom, calls=%fused_computation.113 | custom fusion | flops 147456 | bytes 590336 | tf_op jit(solution)/shard_map/scatter-add | solution.py:134
  424.7 59.5 %fusion.130 = (f32[1,16384]{0,1:T(8,128)}, f32[1,16384]{0,1:T(8,128)}, f32[1,16384]{0,1:T(8,128)}, f32[1,16384]{0,1:T(8,128)}, f32[1,16384]{0,1:T(8,128)}, /*ind...) fusion(f32[9,16384]{0,1:T(8,128)} %scatter_custom_fusion), kind=kLoop, calls=%fused_computation.280 | loop fusion | bytes 1179648 | tf_op jit(solution)/shard_map/transpose(jvp())/unstack | solution.py:52
  546.5 23.0 %all_to_all.19 = f32[14,128,128]{2,0,1:T(8,128)S(1)} all-to-all(f32[14,128,128]{2,0,1:T(8,128)S(1)} %copy.517), channel_id=1, replica_groups=mesh['cx'=8,'cy'=16] {'cx','cy'}, dimensions={1} | all-to-all | bytes 1835008 | tf_op jit(solution)/shard_map/all_to_all | solution.py:94
  (344 shorter events, 140.0 us)
Async XLA Ops:
  2.0 21.2 %all-to-all-start = ((s32[1,128,1]{2,0,1:T(1,128)}), s32[1,128,1]{2,0,1:T(1,128)S(1)}, u32[]{:S(2)}, u32[]{:S(2)}) async-start(s32[1,128,1]{2,0,1:T(1,128)} %copy.487), calls=%async_computation | async-start | bytes 131072 | tf_op jit(solution)/shard_map/all_to_all | solution.py:104
  15.9 16.5 %copy-start.61 = (s32[64]{0:T(128)S(1)}, s32[64]{0:T(128)}, u32[]{:S(2)}) copy-start(s32[64]{0:T(128)} %param.11) | copy-start | bytes 772
  16.0 16.6 %copy-start.60 = (s32[64,2]{0,1:T(2,128)S(1)}, s32[64,2]{0,1:T(2,128)}, u32[]{:S(2)}) copy-start(s32[64,2]{0,1:T(2,128)} %param.12) | copy-start | bytes 1540
  16.0 16.7 %copy-start.57 = (f32[64,3,256]{2,0,1:T(8,128)S(1)}, f32[64,3,256]{2,0,1:T(8,128)}, u32[]{:S(2)}) copy-start(f32[64,3,256]{2,0,1:T(8,128)} %param.13) | copy-start | bytes 589828
  28.1 23.6 %all-to-all-start.1 = ((f32[14,128,128]{2,0,1:T(8,128)}), f32[14,128,128]{2,0,1:T(8,128)S(1)}, u32[]{:S(2)}, u32[]{:S(2)}) async-start(f32[14,128,128]{2,0,1:T(8,128)} %select_bitcast_fusion.1), calls=%async_computation.1 | async-start | bytes 2097152 | tf_op jit(solution)/shard_map/all_to_all | solution.py:90
  51.7 12.9 %copy-start.3 = (f32[14,128,128]{2,0,1:T(8,128)}, f32[14,128,128]{2,0,1:T(8,128)S(1)}, u32[]{:S(2)}) copy-start(f32[14,128,128]{2,0,1:T(8,128)S(1)} %all-to-all-done.1) | copy-start | bytes 2752516
  52.2 12.4 %copy-start.40 = (f32[1,128,128]{2,1,0:T(8,128)}, f32[1,128,128]{2,1,0:T(8,128)S(1)}, u32[]{:S(2)}) copy-start(f32[1,128,128]{2,1,0:T(8,128)S(1)} %add_divide_fusion) | copy-start | bytes 196612
  52.2 6.2 %copy-start.7 = (f32[1,128,128]{2,1,0:T(8,128)}, f32[1,128,128]{2,1,0:T(8,128)S(1)}, u32[]{:S(2)}) copy-start(f32[1,128,128]{2,1,0:T(8,128)S(1)} %multiply_exponential_fusion) | copy-start | bytes 196612
  52.3 6.2 %copy-start.9 = (f32[1,128,128]{2,1,0:T(8,128)}, f32[1,128,128]{2,1,0:T(8,128)S(1)}, u32[]{:S(2)}) copy-start(f32[1,128,128]{2,1,0:T(8,128)S(1)} %multiply_exponential_fusion.1) | copy-start | bytes 196612
  52.3 6.2 %copy-start.14 = (f32[1,128,128]{2,1,0:T(8,128)}, f32[1,128,128]{2,1,0:T(8,128)S(1)}, u32[]{:S(2)}) copy-start(f32[1,128,128]{2,1,0:T(8,128)S(1)} %multiply_exponential_fusion.2) | copy-start | bytes 196612
  52.3 6.1 %copy-start.32 = (f32[1,128,128]{2,1,0:T(8,128)}, f32[1,128,128]{2,1,0:T(8,128)S(1)}, u32[]{:S(2)}) copy-start(f32[1,128,128]{2,1,0:T(8,128)S(1)} %get-tuple-element.391) | copy-start | bytes 196612
  52.3 6.1 %copy-start.34 = (f32[1,128,128]{2,1,0:T(8,128)}, f32[1,128,128]{2,1,0:T(8,128)S(1)}, u32[]{:S(2)}) copy-start(f32[1,128,128]{2,1,0:T(8,128)S(1)} %get-tuple-element.392) | copy-start | bytes 196612
  52.4 6.1 %copy-start.36 = (f32[1,128,128]{2,1,0:T(8,128)}, f32[1,128,128]{2,1,0:T(8,128)S(1)}, u32[]{:S(2)}) copy-start(f32[1,128,128]{2,1,0:T(8,128)S(1)} %get-tuple-element.393) | copy-start | bytes 196612
  52.4 6.1 %copy-start.38 = (f32[1,128,128]{2,1,0:T(8,128)}, f32[1,128,128]{2,1,0:T(8,128)S(1)}, u32[]{:S(2)}) copy-start(f32[1,128,128]{2,1,0:T(8,128)S(1)} %get-tuple-element.394) | copy-start | bytes 196612
  92.8 9.7 %copy-start = (f32[16,256,2,128]{1,3,2,0:T(8,128)}, f32[16,256,2,128]{1,3,2,0:T(8,128)S(1)}, u32[]{:S(2)}) copy-start(f32[16,256,2,128]{1,3,2,0:T(8,128)S(1)} %add_exponential_fusion.2) | copy-start | bytes 12582916 | tf_op jit(solution)/shard_map/while
  102.6 5.8 %copy-start.1 = (f32[16,256,2,128]{1,3,2,0:T(8,128)S(1)}, f32[16,256,2,128]{1,3,2,0:T(8,128)}, u32[]{:S(2)}) copy-start(f32[16,256,2,128]{1,3,2,0:T(8,128)} %copy-done) | copy-start | bytes 12582916 | tf_op jit(solution)/shard_map/while
  102.6 5.8 %copy-start.2 = (f32[16,256,256]{1,2,0:T(8,128)S(1)}, f32[16,256,256]{1,2,0:T(8,128)}, u32[]{:S(2)}) copy-start(f32[16,256,256]{1,2,0:T(8,128)} %get-tuple-element.491) | copy-start | bytes 12582916 | tf_op jit(solution)/shard_map/while
  158.3 9.7 %copy-start = (f32[16,256,2,128]{1,3,2,0:T(8,128)}, f32[16,256,2,128]{1,3,2,0:T(8,128)S(1)}, u32[]{:S(2)}) copy-start(f32[16,256,2,128]{1,3,2,0:T(8,128)S(1)} %add_exponential_fusion.2) | copy-start | bytes 12582916 | tf_op jit(solution)/shard_map/while
  223.8 9.7 %copy-start = (f32[16,256,2,128]{1,3,2,0:T(8,128)}, f32[16,256,2,128]{1,3,2,0:T(8,128)S(1)}, u32[]{:S(2)}) copy-start(f32[16,256,2,128]{1,3,2,0:T(8,128)S(1)} %add_exponential_fusion.2) | copy-start | bytes 12582916 | tf_op jit(solution)/shard_map/while
  233.6 5.8 %copy-start.1 = (f32[16,256,2,128]{1,3,2,0:T(8,128)S(1)}, f32[16,256,2,128]{1,3,2,0:T(8,128)}, u32[]{:S(2)}) copy-start(f32[16,256,2,128]{1,3,2,0:T(8,128)} %copy-done) | copy-start | bytes 12582916 | tf_op jit(solution)/shard_map/while
  233.6 5.8 %copy-start.2 = (f32[16,256,256]{1,2,0:T(8,128)S(1)}, f32[16,256,256]{1,2,0:T(8,128)}, u32[]{:S(2)}) copy-start(f32[16,256,256]{1,2,0:T(8,128)} %get-tuple-element.491) | copy-start | bytes 12582916 | tf_op jit(solution)/shard_map/while
  289.3 9.7 %copy-start = (f32[16,256,2,128]{1,3,2,0:T(8,128)}, f32[16,256,2,128]{1,3,2,0:T(8,128)S(1)}, u32[]{:S(2)}) copy-start(f32[16,256,2,128]{1,3,2,0:T(8,128)S(1)} %add_exponential_fusion.2) | copy-start | bytes 12582916 | tf_op jit(solution)/shard_map/while
  299.1 5.8 %copy-start.1 = (f32[16,256,2,128]{1,3,2,0:T(8,128)S(1)}, f32[16,256,2,128]{1,3,2,0:T(8,128)}, u32[]{:S(2)}) copy-start(f32[16,256,2,128]{1,3,2,0:T(8,128)} %copy-done) | copy-start | bytes 12582916 | tf_op jit(solution)/shard_map/while
  299.1 5.8 %copy-start.2 = (f32[16,256,256]{1,2,0:T(8,128)S(1)}, f32[16,256,256]{1,2,0:T(8,128)}, u32[]{:S(2)}) copy-start(f32[16,256,256]{1,2,0:T(8,128)} %get-tuple-element.491) | copy-start | bytes 12582916 | tf_op jit(solution)/shard_map/while
  327.2 6.0 %copy-start.62 = (f32[4,16,3,256]{3,1,0,2:T(8,128)}, f32[4,16,3,256]{3,1,0,2:T(8,128)S(1)}, u32[]{:S(2)}) copy-start(f32[4,16,3,256]{3,1,0,2:T(8,128)S(1)} %get-tuple-element.137) | copy-start | bytes 589828
  526.8 9.9 %copy-start.55 = (f32[1,16384]{1,0:T(1,128)S(1)}, f32[1,16384]{1,0:T(1,128)}, u32[]{:S(2)}) copy-start(f32[1,16384]{1,0:T(1,128)} %get-tuple-element.310) | copy-start | bytes 196612
  526.8 9.9 %copy-start.56 = (f32[1,16384]{1,0:T(1,128)S(1)}, f32[1,16384]{1,0:T(1,128)}, u32[]{:S(2)}) copy-start(f32[1,16384]{1,0:T(1,128)} %get-tuple-element.315) | copy-start | bytes 196612
  532.2 5.9 %copy-start.52 = (f32[1,16384]{1,0:T(1,128)S(1)}, f32[1,16384]{1,0:T(1,128)}, u32[]{:S(2)}) copy-start(f32[1,16384]{1,0:T(1,128)} %get-tuple-element.311) | copy-start | bytes 196612
  532.3 5.9 %copy-start.53 = (f32[1,16384]{1,0:T(1,128)S(1)}, f32[1,16384]{1,0:T(1,128)}, u32[]{:S(2)}) copy-start(f32[1,16384]{1,0:T(1,128)} %get-tuple-element.317) | copy-start | bytes 196612
  532.3 5.9 %copy-start.54 = (f32[1,16384]{1,0:T(1,128)S(1)}, f32[1,16384]{1,0:T(1,128)}, u32[]{:S(2)}) copy-start(f32[1,16384]{1,0:T(1,128)} %get-tuple-element.332) | copy-start | bytes 196612
  532.3 6.3 %copy-start.41 = (f32[1,128,128]{2,1,0:T(8,128)S(1)}, f32[1,128,128]{2,1,0:T(8,128)}, u32[]{:S(2)}) copy-start(f32[1,128,128]{2,1,0:T(8,128)} %copy-done.40) | copy-start | bytes 196612
  545.7 23.9 %copy-start.59 = (s32[128]{0:T(128)S(1)}, s32[128]{0:T(128)}, u32[]{:S(2)}) copy-start(s32[128]{0:T(128)} %copy-done.58) | copy-start | bytes 1540
  (42 other events, 219.5 us)
where the time goes:
time: 580 us; the launch traced here: 572 us
  other arithmetic  198 us (34%)
  local copies, waits for them, and re-layouts  188 us (32%)
  matrix products  118 us (20%)
  waiting for transfers between devices  25.6 us (4%)
  blocking collectives  23 us (4%)
  starting transfers between devices  15.8 us (3%)
    scatter-add x1, other arithmetic, per_device(): jnp.zeros((9, feats.shape[1]), jnp.float32).at[:, lists.reshape(-1)]  91.4 us
    dot_general x12, matrix products, tile_image(): jnp.einsum('ck,pk->cp', features[6:9], weight, precision=lax.Precision.HI...  61.3 us
    another operation x2, local copies, waits for them, and re-layouts, project(): jnp.stack([focal * xpos / depth, focal * ypos / depth, cov_c / determ, -c...  60.5 us
    unnamed x137, local copies, waits for them, and re-layouts  59.3 us
    gather x8, local copies, waits for them, and re-layouts, per_tile(): gathered = jnp.take(feats, entries, axis=1)  59.1 us
    dot_general x8, matrix products, tile_image(): jnp.einsum('pbk,kj->pbj', pieces, strict, precision=lax.Precision.HIGHEST)  55.3 us
    reduce_sum x4, other arithmetic, tile_image(): features[3] * delta_x * delta_y  37.2 us
    mul x4, other arithmetic, tile_image(): alpha = jnp.minimum(0.99, features[5] * jnp.exp(power)) * live[None, :]  23.6 us
  transfers between devices with their start and end apart: 2, of which 2 were waited for; matrix products, arithmetic and copies ran while one was open for 1% of the time, Pallas kernels for 0%

commit v1 on v0

v1 whole, which is shorter than its diff:
```python
import functools

import jax
import jax.numpy as jnp
import numpy as np
from jax import lax
from jax.experimental import pallas as pl
from jax.experimental.pallas import tpu as pltpu
from jax.sharding import PartitionSpec as P

SIDE = 16
PIX = SIDE * SIDE
FOCAL = 1100.0
LANES = 128
TG = 8
NFEAT = 9
NPAR = 14
LOG2E = 1.4426950408889634
bf16 = jnp.bfloat16
f32 = jnp.float32
NT_DIMS = (((1,), (1,)), ((), ()))
AXES = ("cx", "cy")


def geometry(params):
    focal = jnp.float32(FOCAL)
    xpos, ypos, depth = params[0], params[1], params[2]
    svar = [jnp.exp(2.0 * params[3 + i]) for i in range(3)]
    qnorm = jnp.sqrt(params[6] ** 2 + params[7] ** 2 + params[8] ** 2 + params[9] ** 2)
    qw, qx, qy, qz = (params[6] / qnorm, params[7] / qnorm, params[8] / qnorm, params[9] / qnorm)
    rot = [
        [1.0 - 2.0 * (qy * qy + qz * qz), 2.0 * (qx * qy - qw * qz), 2.0 * (qx * qz + qw * qy)],
        [2.0 * (qx * qy + qw * qz), 1.0 - 2.0 * (qx * qx + qz * qz), 2.0 * (qy * qz - qw * qx)],
        [2.0 * (qx * qz - qw * qy), 2.0 * (qy * qz + qw * qx), 1.0 - 2.0 * (qx * qx + qy * qy)],
    ]

    def sigma(i, j):
        return (
            rot[i][0] * rot[j][0] * svar[0]
            + rot[i][1] * rot[j][1] * svar[1]
            + rot[i][2] * rot[j][2] * svar[2]
        )

    j_diag = focal / depth
    j_xz = -focal * xpos / (depth * depth)
    j_yz = -focal * ypos / (depth * depth)
    s02, s12, s22 = sigma(0, 2), sigma(1, 2), sigma(2, 2)
    cov_a = j_diag * j_diag * sigma(0, 0) + 2.0 * j_diag * j_xz * s02 + j_xz * j_xz * s22 + 0.3
    cov_b = (
        j_diag * j_diag * sigma(0, 1)
        + j_diag * j_yz * s02
        + j_xz * j_diag * s12
        + j_xz * j_yz * s22
    )
    cov_c = j_diag * j_diag * sigma(1, 1) + 2.0 * j_diag * j_yz * s12 + j_yz * j_yz * s22 + 0.3
    determ = cov_a * cov_c - cov_b * cov_b
    return (
        focal * xpos / depth,
        focal * ypos / depth,
        cov_c / determ,
        -cov_b / determ,
        cov_a / determ,
    )


def stage_blocks(params_ref, asked_ref, stage, blocks):
    @pl.loop(0, blocks, unroll=8)
    def _(r):
        col = pl.multiple_of(asked_ref[r] * LANES, LANES)
        stage[pl.ds(pl.multiple_of(r * 16, 16), NPAR), :] = params_ref[:, pl.ds(col, LANES)]


def project_kernel(params_ref, out_ref, stage):
    blocks = out_ref.shape[0]

    @pl.loop(0, blocks, unroll=8)
    def _(r):
        col = pl.multiple_of(r * LANES, LANES)
        stage[pl.ds(pl.multiple_of(r * 16, 16), NPAR), :] = params_ref[:, pl.ds(col, LANES)]

    @pl.loop(0, blocks // 8)
    def _(i):
        par = [stage[pl.ds(i * 128 + c, 8, stride=16), :] for c in range(NPAR)]
        feats = list(geometry(par))
        feats.append(-jnp.log(1.0 + jnp.exp(-par[10])))
        feats += par[11:14]
        for c in range(NFEAT):
            stage[pl.ds(i * 128 + c, 8, stride=16), :] = feats[c]

    @pl.loop(0, blocks, unroll=8)
    def _(r):
        out_ref[r] = stage[pl.ds(pl.multiple_of(r * 16, 16), NFEAT), :]


def place(device):
    minor = lax.axis_size("cy")
    return (device // minor, lax.rem(device, minor))


def position():
    return lax.axis_index("cx") * lax.axis_size("cy") + lax.axis_index("cy")


def greet(peers):
    me = position()
    barrier = pltpu.get_barrier_semaphore()

    @pl.loop(1, peers)
    def _(off):
        pl.semaphore_signal(
            barrier,
            inc=1,
            device_id=place(lax.rem(me + off, peers)),
            device_id_type=pl.DeviceIdType.MESH,
        )

    pl.semaphore_wait(barrier, peers - 1)


def exchange(source, target, send_sem, recv_sem, peers, fill=None):
    me = position()

    @pl.loop(1, peers)
    def _(off):
        peer = lax.rem(me + off, peers)
        if fill is not None:
            fill(peer)
        pltpu.make_async_remote_copy(
            src_ref=source.at[peer],
            dst_ref=target.at[me],
            send_sem=send_sem,
            recv_sem=recv_sem,
            device_id=place(peer),
            device_id_type=pl.DeviceIdType.MESH,
        ).start()

    if fill is not None:
        fill(me)
    target[me] = source[me]
    rest = pltpu.make_async_remote_copy(
        src_ref=source.at[pl.ds(0, peers - 1)],
        dst_ref=target.at[pl.ds(0, peers - 1)],
        send_sem=send_sem,
        recv_sem=recv_sem,
        device_id=place(lax.rem(me + 1, peers)),
        device_id_type=pl.DeviceIdType.MESH,
    )
    rest.wait_send()
    rest.wait_recv()


def fetch_kernel(
    req_ref, table_ref, out_ref, asked_ref, asked_v, asked_s, outgoing, send1, recv1, send2, recv2, local
):
    peers = table_ref.shape[0]
    greet(peers)
    exchange(req_ref, asked_v, send1, recv1, peers)
    copy = pltpu.make_async_copy(asked_v, asked_s, local)
    copy.start()
    copy.wait()
    asked_ref[...] = asked_v[...]

    def fill(peer):
        outgoing[peer] = table_ref[asked_s[peer, 0, 0]]

    exchange(outgoing, out_ref, send2, recv2, peers, fill)


def return_kernel(grad_ref, out_ref, send, recv):
    peers = grad_ref.shape[0]
    greet(peers)
    exchange(grad_ref, out_ref, send, recv, peers)


def unproject_kernel(params_ref, asked_ref, grad_ref, out_ref, stage):
    blocks = grad_ref.shape[0]
    stage_blocks(params_ref, asked_ref, stage, blocks)

    @pl.loop(0, blocks // 8)
    def _(i):
        par = [stage[pl.ds(i * 128 + c, 8, stride=16), :] for c in range(NPAR)]
        rows = pl.ds(pl.multiple_of(i * 8, 8), 8)
        grad = [grad_ref[rows, c, :] for c in range(NFEAT)]
        _, pull = jax.vjp(geometry, par[:10])
        res = list(pull(tuple(grad[:5]))[0])
        decay = jnp.exp(-par[10])
        res.append(grad[5] * (decay / (1.0 + decay)))
        res += grad[6:9]
        for c in range(NPAR):
            stage[pl.ds(i * 128 + c, 8, stride=16), :] = res[c]

    @pl.loop(0, blocks, unroll=8)
    def _(r):
        col = pl.multiple_of(asked_ref[r] * LANES, LANES)
        out_ref[:, pl.ds(col, LANES)] = stage[pl.ds(pl.multiple_of(r * 16, 16), NPAR), :]


def split(x, parts):
    out = []
    for _ in range(parts - 1):
        p = x.astype(bf16)
        out.append(p)
        x = x - p.astype(f32)
    out.append(x.astype(bf16))
    return out


def render_kernel(
    feat_ref, idx_ref, len_ref, ox_ref, oy_ref, cot_ref, mono_ref,
    img_ref, gf_ref,
    tab3, tab2, picked, lhs, qg, alpha, wmask, whi, wlo, dqhi, dqlo, colt, scat, rhs_sc, acc,
):
    groups, span = idx_ref.shape
    length = span // TG
    owners = feat_ref.shape[0]
    half = LANES // 2
    for c in range(NFEAT):
        xt = feat_ref[:, c, :].T
        rem = jnp.concatenate([xt[:half], xt[half:]], axis=1)
        for s, p in enumerate(split(rem, 3 if c < 2 else 2)):
            cols = slice(s * 2 * owners, (s + 1) * 2 * owners)
            if c < 2:
                tab3[c * half : (c + 1) * half, cols] = p
            else:
                tab2[(c - 2) * half : (c - 1) * half, cols] = p
    acc[...] = jnp.zeros_like(acc)
    part = 1024
    kio = lax.broadcasted_iota(jnp.int32, (2 * owners, part), 0)
    lio = lax.broadcasted_iota(jnp.int32, (half, part), 0)
    own = (lax.broadcasted_iota(jnp.int32, (TG, span), 0)) == (
        lax.broadcasted_iota(jnp.int32, (TG, span), 1) % TG
    )
    entry = lax.broadcasted_iota(jnp.int32, (1, span), 1) // TG
    mono = mono_ref[...]
    mono_b = mono.astype(bf16)

    @pl.loop(0, groups)
    def _(g):
        for t in range(span // part):
            idx = idx_ref[pl.ds(g, 1), t * part : (t + 1) * part]
            hi = ((idx >> 6) & 1) * owners + (idx >> 7)
            lo = idx & (half - 1)
            oh = jnp.where(kio == hi, 1.0, 0.0).astype(bf16)
            mine = lio == lo
            t3 = jnp.dot(
                tab3[...], jnp.concatenate([oh, oh, oh], axis=0), preferred_element_type=f32
            )
            t2 = jnp.dot(tab2[...], jnp.concatenate([oh, oh], axis=0), preferred_element_type=f32)
            for c in range(NFEAT):
                v = t3[c * half : (c + 1) * half] if c < 2 else t2[(c - 2) * half : (c - 1) * half]
                picked[c : c + 1, t * part : (t + 1) * part] = jnp.sum(
                    jnp.where(mine, v, 0.0), axis=0, keepdims=True
                )
        f = [picked[c : c + 1, :] for c in range(NFEAT)]
        live = entry < len_ref[pl.ds(g, 1), :]
        u = f[0] - ox_ref[pl.ds(g, 1), :]
        v = f[1] - oy_ref[pl.ds(g, 1), :]
        a, b, c2 = f[2], f[3], f[4]
        pu = a * u + b * v
        pv = c2 * v + b * u
        k0 = f[5] - 0.5 * (u * pu + v * pv)
        coef = [
            jnp.where(live, LOG2E * k0, -1e30),
            jnp.where(live, LOG2E * pu, 0.0),
            jnp.where(live, LOG2E * pv, 0.0),
            jnp.where(live, (-0.5 * LOG2E) * a, 0.0),
            jnp.where(live, -LOG2E * b, 0.0),
            jnp.where(live, (-0.5 * LOG2E) * c2, 0.0),
            jnp.zeros_like(u),
            jnp.zeros_like(u),
        ]
        coef = jnp.concatenate(coef, axis=0)
        rows = [p.astype(f32) for p in split(coef, 3)]
        rows.append(jnp.zeros((8, span), f32))
        col_hi, col_lo = [], []
        for c in range(3):
            h, l = split(f[6 + c], 2)
            col_hi.append(jnp.where(own, h.astype(f32), 0.0))
            col_lo.append(jnp.where(own, l.astype(f32), 0.0))
        rows += col_hi + col_hi + col_lo
        left = jnp.concatenate(rows + [jnp.zeros((24, span), f32)], axis=0)
        colt[...] = left[32:128].astype(bf16)
        for q in range(span // LANES):
            lhs[q * LANES : (q + 1) * LANES, :] = left[:, q * LANES : (q + 1) * LANES].T.astype(bf16)
        cot = jnp.concatenate(
            [
                jnp.concatenate(
                    [cot_ref[pl.ds(g * 6 * TG + 2 * c + h, TG, stride=6), :] for h in range(2)],
                    axis=1,
                )
                for c in range(3)
            ],
            axis=0,
        )
        cot_hi, cot_lo = split(cot, 2)
        right_q = jnp.concatenate([mono_b[:8]] * 3 + [jnp.zeros((8 + 96, PIX), bf16)], axis=0)
        right_g = jnp.concatenate(
            [jnp.zeros((32, PIX), bf16), cot_hi, cot_lo, cot_hi, jnp.zeros((24, PIX), bf16)], axis=0
        )
        qg[...] = jnp.dot(
            lhs[...], jnp.concatenate([right_q, right_g], axis=1), preferred_element_type=f32
        )

        def fwd(i, trans):
            base = pl.multiple_of(i * 128, 128)
            for s in range(8):
                ws = []
                for h in range(2):
                    at = pl.ds(base + s * 16 + h * 8, 8)
                    e = jnp.exp2(qg[at, :PIX])
                    al = jnp.minimum(e, 0.99)
                    w = al * trans
                    trans = trans - w
                    alpha[at, :] = al
                    wmask[at, :] = jnp.where(e < 0.99, w, 0.0)
                    ws.append(w)
                w2 = jnp.concatenate(ws, axis=0)
                w2h, w2l = split(w2, 2)
                at2 = pl.ds(base + s * 16, 16)
                whi[at2, :] = w2h
                wlo[at2, :] = w2l
            return trans

        lax.fori_loop(0, length // 16, fwd, jnp.ones((TG, PIX), f32))

        def bwd(n, behind):
            i = length // 16 - 1 - n
            base = pl.multiple_of(i * 128, 128)
            for s in reversed(range(8)):
                ds = [None, None]
                for h in (1, 0):
                    at = pl.ds(base + s * 16 + h * 8, 8)
                    d = qg[at, PIX:] - behind
                    behind = behind + alpha[at, :] * d
                    ds[h] = wmask[at, :] * d
                d2h, d2l = split(jnp.concatenate(ds, axis=0), 2)
                at2 = pl.ds(base + s * 16, 16)
                dqhi[at2, :] = d2h
                dqlo[at2, :] = d2l
            return behind

        lax.fori_loop(0, length // 16, bwd, jnp.zeros((TG, PIX), f32))

        ch, cl = colt[0:24, :], colt[48:72, :]
        img = jnp.dot(jnp.concatenate([ch, cl], axis=0), whi[...], preferred_element_type=f32)
        img = img[:24] + img[24:] + jnp.dot(ch, wlo[...], preferred_element_type=f32)
        for c in range(3):
            for h in range(2):
                img_ref[pl.ds(g * 6 * TG + 2 * c + h, TG, stride=6), :] = img[
                    c * TG : (c + 1) * TG, h * LANES : (h + 1) * LANES
                ]
        both = jnp.concatenate([cot_hi, cot_lo], axis=0)
        dcol = lax.dot_general(both, whi[...], NT_DIMS, preferred_element_type=f32)
        dcol = (
            dcol[:24] + dcol[24:]
            + lax.dot_general(cot_hi, wlo[...], NT_DIMS, preferred_element_type=f32)
        )
        mom = lax.dot_general(mono_b, dqhi[...], NT_DIMS, preferred_element_type=f32)
        mom = mom + lax.dot_general(mono_b, dqlo[...], NT_DIMS, preferred_element_type=f32)
        s0, sx, sy = mom[0:1], mom[1:2], mom[2:3]
        sxx, sxy, syy = mom[3:4], mom[4:5], mom[5:6]
        mx = sx - u * s0
        my = sy - v * s0
        mxx = sxx - u * (sx + mx)
        myy = syy - v * (sy + my)
        mxy = sxy - u * sy - v * mx
        out = [
            a * mx + b * my,
            c2 * my + b * mx,
            -0.5 * mxx,
            -mxy,
            -0.5 * myy,
            s0,
        ]
        for c in range(3):
            out.append(
                jnp.sum(jnp.where(own, dcol[c * TG : (c + 1) * TG], 0.0), axis=0, keepdims=True)
            )

        idx = idx_ref[pl.ds(g, 1), :]
        hio = lax.broadcasted_iota(jnp.int32, (owners // 2, span), 0)
        loo = lax.broadcasted_iota(jnp.int32, (2 * LANES, span), 0)
        hi = (idx >> 7) & (owners // 2 - 1)
        lo = ((idx >> 13) << 7) | (idx & (LANES - 1))
        oh = jnp.where(hio == hi, 1.0, 0.0).astype(bf16)
        ol = jnp.where(loo == lo, 1.0, 0.0).astype(bf16)
        rhs_sc[:, :span] = ol
        rhs_sc[:, span:] = ol
        hh = owners // 2
        for c in range(NFEAT):
            for s, p in enumerate(split(out[c], 2)):
                scat[c * hh : (c + 1) * hh, s * span : (s + 1) * span] = oh * p
        acc[...] += lax.dot_general(scat[...], rhs_sc[...], NT_DIMS, preferred_element_type=f32)

    hh = owners // 2
    for c in range(NFEAT):
        gf_ref[:hh, c, :] = acc[c * hh : (c + 1) * hh, :LANES]
        gf_ref[hh:, c, :] = acc[c * hh : (c + 1) * hh, LANES:]


def monomials():
    pix = np.arange(PIX)
    x = (pix % SIDE) - (SIDE - 1) / 2.0
    y = (pix // SIDE) - (SIDE - 1) / 2.0
    one = np.ones(PIX)
    return np.stack([one, x, y, x * x, x * y, y * y, 0 * one, 0 * one]).astype(np.float32)


VM = pl.BlockSpec(memory_space=pltpu.VMEM)
SM = pl.BlockSpec(memory_space=pltpu.SMEM)
LIMIT = pltpu.CompilerParams(vmem_limit_bytes=56 * 1024 * 1024)


def per_device(params, requests, lists, list_len, offsets, cotangent):
    peers = lax.axis_size(AXES)
    g_dev = params.shape[1]
    tiles, length = lists.shape
    groups = tiles // TG
    span = TG * length
    table = pl.pallas_call(
        project_kernel,
        out_shape=jax.ShapeDtypeStruct((peers, NFEAT, LANES), f32),
        in_specs=[VM],
        out_specs=VM,
        scratch_shapes=[pltpu.VMEM((peers * 16, LANES), f32)],
        compiler_params=LIMIT,
        name="project",
    )(params)
    wanted = jnp.broadcast_to(requests.reshape(peers, 1, 1), (peers, 1, LANES))
    fetched, asked = pl.pallas_call(
        fetch_kernel,
        out_shape=(
            jax.ShapeDtypeStruct((peers, NFEAT, LANES), f32),
            jax.ShapeDtypeStruct((peers, 1, LANES), jnp.int32),
        ),
        in_specs=[VM, VM],
        out_specs=(VM, VM),
        scratch_shapes=[
            pltpu.VMEM((peers, 1, LANES), jnp.int32),
            pltpu.SMEM((peers, 1, LANES), jnp.int32),
            pltpu.VMEM((peers, NFEAT, LANES), f32),
        ]
        + [pltpu.SemaphoreType.DMA] * 5,
        compiler_params=pltpu.CompilerParams(
            collective_id=0, has_side_effects=True, vmem_limit_bytes=32 * 1024 * 1024
        ),
        name="fetch",
    )(wanted, table)
    asked = asked[:, 0, 0]

    idx = lists.reshape(groups, TG, length).transpose(0, 2, 1).reshape(groups, span)
    lens = jnp.tile(list_len.reshape(groups, TG), (1, length))
    centre = (offsets * SIDE + SIDE // 2).astype(f32)
    ox = jnp.tile(centre[:, 0].reshape(groups, TG), (1, length))
    oy = jnp.tile(centre[:, 1].reshape(groups, TG), (1, length))
    image, gfeat = pl.pallas_call(
        render_kernel,
        out_shape=(
            jax.ShapeDtypeStruct((tiles * 6, LANES), f32),
            jax.ShapeDtypeStruct((peers, NFEAT, LANES), f32),
        ),
        in_specs=[VM] * 7,
        out_specs=(VM, VM),
        scratch_shapes=[
            pltpu.VMEM((LANES, 6 * peers), bf16),
            pltpu.VMEM((7 * LANES // 2, 4 * peers), bf16),
            pltpu.VMEM((16, span), f32),
            pltpu.VMEM((span, LANES), bf16),
            pltpu.VMEM((span, 2 * PIX), f32),
            pltpu.VMEM((span, PIX), f32),
            pltpu.VMEM((span, PIX), f32),
            pltpu.VMEM((span, PIX), bf16),
            pltpu.VMEM((span, PIX), bf16),
            pltpu.VMEM((span, PIX), bf16),
            pltpu.VMEM((span, PIX), bf16),
            pltpu.VMEM((96, span), bf16),
            pltpu.VMEM((NFEAT * peers // 2, 2 * span), bf16),
            pltpu.VMEM((2 * LANES, 2 * span), bf16),
            pltpu.VMEM((NFEAT * peers // 2, 2 * LANES), f32),
        ],
        compiler_params=LIMIT,
        name="render",
    )(fetched, idx, lens, ox, oy, cotangent.reshape(tiles * 6, LANES), jnp.asarray(monomials()))

    landed = pl.pallas_call(
        return_kernel,
        out_shape=jax.ShapeDtypeStruct((peers, NFEAT, LANES), f32),
        in_specs=[VM],
        out_specs=VM,
        scratch_shapes=[pltpu.SemaphoreType.DMA] * 2,
        compiler_params=pltpu.CompilerParams(
            collective_id=1, has_side_effects=True, vmem_limit_bytes=32 * 1024 * 1024
        ),
        name="give_back",
    )(gfeat)
    grads = pl.pallas_call(
        unproject_kernel,
        out_shape=jax.ShapeDtypeStruct((NPAR, g_dev), f32),
        in_specs=[VM, SM, VM],
        out_specs=VM,
        scratch_shapes=[pltpu.VMEM((peers * 16, LANES), f32)],
        compiler_params=LIMIT,
        name="unproject",
    )(params, asked, landed)
    return image.reshape(tiles, 3, PIX), grads


def solution(mesh):
    in_specs = (
        P(None, AXES),
        P(AXES, None, None),
        P(AXES, None),
        P(AXES),
        P(AXES, None),
        P(AXES, None, None),
    )
    out_specs = (P(AXES, None, None), P(None, AXES))
    return jax.shard_map(
        per_device, mesh=mesh, in_specs=in_specs, out_specs=out_specs, check_vma=False
    )
```

time: 580 us -> 144 us (0.25); the launches traced: 572 us -> 144 us
  other arithmetic: 198 us -> 0.01 us
  local copies, waits for them, and re-layouts: 188 us -> 18.4 us
  Pallas kernels: 0 us -> 125 us
  matrix products: 118 us -> 0 us
  waiting for transfers between devices: 25.6 us -> 0 us
  blocking collectives: 23 us -> 0 us
  starting transfers between devices: 15.8 us -> 0 us
    pallas_call x0 -> x5, Pallas kernels: none -> 125 us  [the longest x1 69.7 us: per_device(): pl.pallas_call(render_kernel, out_shape=(jax.ShapeDtypeStruct((tiles * 6,...]
    dot_general x21 -> x0, matrix products: 118 us -> none  [the longest x12 61.3 us: tile_image(): jnp.einsum('ck,pk->cp', features[6:9], weight, precision=lax.Precision.HI...]
    scatter-add x1 -> x0, other arithmetic: 91.4 us -> none  [per_device(): jnp.zeros((9, feats.shape[1]), jnp.float32).at[:, lists.reshape(-1)]]
    gather x9 -> x0, local copies, waits for them, and re-layouts: 59.8 us -> none  [the longest x8 59.1 us: per_tile(): gathered = jnp.take(feats, entries, axis=1)]
    another operation x2 -> x9, local copies, waits for them, and re-layouts: 60.5 us -> 3.87 us  [the longest x3 1.3 us: per_device(): oy = jnp.tile(centre[:, 1].reshape(groups, TG), (1, length))]
    reduce_sum x8 -> x0, other arithmetic: 54.8 us -> none  [the longest x4 37.2 us: tile_image(): features[3] * delta_x * delta_y]
    unnamed x137 -> x18, local copies, waits for them, and re-layouts: 59.3 us -> 8 us
    mul x15 -> x0, other arithmetic: 28 us -> none  [the longest x4 23.6 us: tile_image(): alpha = jnp.minimum(0.99, features[5] * jnp.exp(power)) * live[None, :]]
  transfers between devices with their start and end apart: 2 -> 0, of which waited for: 2 -> 0; matrix products, arithmetic and copies ran while one was open for 1% -> 0% of each run, Pallas kernels for 0% -> 0%
where the time goes in v1:
time: 144 us
  Pallas kernels  125 us (87%)
  local copies, waits for them, and re-layouts  18.4 us (13%)
    pallas_call x1, Pallas kernels, per_device(): pl.pallas_call(render_kernel, out_shape=(jax.ShapeDtypeStruct((tiles * 6,...  69.7 us
    pallas_call x1, Pallas kernels, per_device(): pl.pallas_call(fetch_kernel, out_shape=(jax.ShapeDtypeStruct((peers, NFEA...  29.6 us
    pallas_call x1, Pallas kernels, per_device(): pl.pallas_call(return_kernel, out_shape=jax.ShapeDtypeStruct((peers, NFEA...  16.9 us
    unnamed x18, local copies, waits for them, and re-layouts  8 us
    pallas_call x1, Pallas kernels, per_device(): pl.pallas_call(unproject_kernel, out_shape=jax.ShapeDtypeStruct((NPAR, g_...  5 us
    pallas_call x1, Pallas kernels, per_device(): pl.pallas_call(project_kernel, out_shape=jax.ShapeDtypeStruct((peers, NFE...  3.47 us
    slice x1, local copies, waits for them, and re-layouts, per_device(): asked = asked[:, 0, 0]  3.04 us

profile of v1, /device:TPU:1, one launch (start us, length us, event | category | flops | bytes accessed | tf_op | source)
XLA Modules:
  0.0 143.8 jit_solution(5956097663992537416)
XLA Ops:
  0.6 0.7 copy-done.5
  1.3 0.1 tile.36
  1.4 0.1 tile.33
  1.5 0.6 copy-done.7
  2.1 0.1 tile.30
  2.2 0.6 copy-done.6
  2.7 0.2 broadcast_in_dim.8.req_ref
  2.9 1.1 copy.13
  4.0 0.8 reshape.34.cot_ref
  4.8 0.1 tile.31
  4.9 1.1 tile.32.len_ref
  6.0 0.1 tile.34
  6.1 1.1 tile.35.ox_ref
  7.2 0.1 tile.37
  7.3 0.0 copy-start.4
  7.3 1.1 tile.38.oy_ref
  8.4 0.0 copy-done.4
  8.5 0.3 copy.12
  8.8 1.1 reshape.33.idx_ref
  9.9 3.5 %project.1.table_ref = f32[128,9,128]{2,1,0:T(8,128)} custom-call(f32[14,16384]{1,0:T(8,128)} %params_ref.3), custom_call_target="tpu_custom_call" | custom-call | tf_op jit(solution)/shard_map/project/pallas_call | solution.py:420
  13.4 1.2 copy-done
  14.6 29.6 %fetch.1 = (f32[128,9,128]{2,1,0:T(8,128)S(1)}, s32[128,1,128]{2,1,0:T(1,128)S(1)}) custom-call(s32[128,1,128]{2,1,0:T(1,128)S(1)} %broadcast_in_dim.8.req_ref, f32[128,9,128]{2,1,0:T(8,128)S(1)} %copy-done), custom_call_target="tpu_custom_call" | custom-call | tf_op jit(solution)/shard_map/fetch/pallas_call | solution.py:430
  44.2 0.0 copy-start.3
  44.2 1.0 copy-done.3
  45.2 69.7 %render.1 = (f32[384,128]{1,0:T(8,128)}, f32[128,9,128]{2,1,0:T(8,128)}) custom-call(f32[128,9,128]{2,1,0:T(8,128)} %copy-done.3, s32[8,2048]{1,0:T(8,128)} %reshape.33.idx_ref, s32[8,2048]{1,0:T(8,128)} %tile.32.len_ref, f32[8,2048]{1,0:T(8,128)} %tile.35.ox_ref, f32[8,2048]{1,0:T(8,128)} %tile.38.oy_ref, f32[384,128]{1,0:T(8,128)} %reshape.34.cot_ref, ...), custom_call_target="tpu_custom_call" | custom-call | tf_op jit(solution)/shard_map/render/pallas_call | solution.py:456
  114.9 3.0 %slice_reduce_fusion.asked_ref = s32[128]{0:T(128)} fusion(s32[128,1,128]{2,1,0:T(1,128)S(1)} %get-tuple-element.8), kind=kLoop, calls=%fused_computation | loop fusion | bytes 1024 | tf_op jit(solution)/shard_map/slice | solution.py:449
  117.9 1.0 reshape.35
  119.0 0.7 copy.14
  119.7 1.2 copy-done.2
  120.9 16.9 %give_back.1.grad_ref = f32[128,9,128]{2,1,0:T(8,128)S(1)} custom-call(f32[128,9,128]{2,1,0:T(8,128)S(1)} %copy-done.2), custom_call_target="tpu_custom_call" | custom-call | tf_op jit(solution)/shard_map/give_back/pallas_call | solution.py:485
  137.8 1.0 copy-done.1
  138.8 5.0 %unproject.1 = f32[14,16384]{1,0:T(8,128)} custom-call(f32[14,16384]{1,0:T(8,128)} %params_ref.3, s32[128]{0:T(128)} %slice_reduce_fusion.asked_ref, f32[128,9,128]{2,1,0:T(8,128)} %copy-done.1), custom_call_target="tpu_custom_call" | custom-call | tf_op jit(solution)/shard_map/unproject/pallas_call | solution.py:496
  (8 shorter events, 0.0 us)
Async XLA Ops:
  0.6 0.7 copy-start.5
  1.4 0.7 copy-start.7
  2.1 0.7 copy-start.6
  7.3 1.2 copy-start.4
  13.4 1.2 copy-start
  44.2 1.0 copy-start.3
  119.7 1.2 copy-start.2
  137.8 1.0 copy-start.1

commit v2 on v0

v2 whole, which is shorter than its diff:
```python
import functools

import jax
import jax.numpy as jnp
import numpy as np
from jax import lax
from jax.experimental import pallas as pl
from jax.experimental.pallas import tpu as pltpu
from jax.sharding import PartitionSpec as P

SIDE = 16
PIX = SIDE * SIDE
FOCAL = 1100.0
LANES = 128
TG = 8
NFEAT = 9
NPAR = 14
LOG2E = 1.4426950408889634
NT_DIMS = (((1,), (1,)), ((), ()))
bf16 = jnp.bfloat16
f32 = jnp.float32
AXES = ("cx", "cy")


def geometry(params):
    focal = jnp.float32(FOCAL)
    xpos, ypos, depth = params[0], params[1], params[2]
    svar = [jnp.exp(2.0 * params[3 + i]) for i in range(3)]
    qnorm = jnp.sqrt(params[6] ** 2 + params[7] ** 2 + params[8] ** 2 + params[9] ** 2)
    qw, qx, qy, qz = (params[6] / qnorm, params[7] / qnorm, params[8] / qnorm, params[9] / qnorm)
    rot = [
        [1.0 - 2.0 * (qy * qy + qz * qz), 2.0 * (qx * qy - qw * qz), 2.0 * (qx * qz + qw * qy)],
        [2.0 * (qx * qy + qw * qz), 1.0 - 2.0 * (qx * qx + qz * qz), 2.0 * (qy * qz - qw * qx)],
        [2.0 * (qx * qz - qw * qy), 2.0 * (qy * qz + qw * qx), 1.0 - 2.0 * (qx * qx + qy * qy)],
    ]

    def sigma(i, j):
        return (
            rot[i][0] * rot[j][0] * svar[0]
            + rot[i][1] * rot[j][1] * svar[1]
            + rot[i][2] * rot[j][2] * svar[2]
        )

    j_diag = focal / depth
    j_xz = -focal * xpos / (depth * depth)
    j_yz = -focal * ypos / (depth * depth)
    s02, s12, s22 = sigma(0, 2), sigma(1, 2), sigma(2, 2)
    cov_a = j_diag * j_diag * sigma(0, 0) + 2.0 * j_diag * j_xz * s02 + j_xz * j_xz * s22 + 0.3
    cov_b = (
        j_diag * j_diag * sigma(0, 1)
        + j_diag * j_yz * s02
        + j_xz * j_diag * s12
        + j_xz * j_yz * s22
    )
    cov_c = j_diag * j_diag * sigma(1, 1) + 2.0 * j_diag * j_yz * s12 + j_yz * j_yz * s22 + 0.3
    determ = cov_a * cov_c - cov_b * cov_b
    return (
        focal * xpos / depth,
        focal * ypos / depth,
        cov_c / determ,
        -cov_b / determ,
        cov_a / determ,
    )


def stage_blocks(params_ref, asked_ref, stage, blocks):
    @pl.loop(0, blocks, unroll=8)
    def _(r):
        col = pl.multiple_of(asked_ref[r] * LANES, LANES)
        stage[pl.ds(pl.multiple_of(r * 16, 16), NPAR), :] = params_ref[:, pl.ds(col, LANES)]


def project(params_ref, out_ref, stage):
    blocks = out_ref.shape[0]

    @pl.loop(0, blocks, unroll=8)
    def _(r):
        col = pl.multiple_of(r * LANES, LANES)
        stage[pl.ds(pl.multiple_of(r * 16, 16), NPAR), :] = params_ref[:, pl.ds(col, LANES)]

    @pl.loop(0, blocks // 8)
    def _(i):
        par = [stage[pl.ds(i * 128 + c, 8, stride=16), :] for c in range(NPAR)]
        feats = list(geometry(par))
        feats.append(-jnp.log(1.0 + jnp.exp(-par[10])))
        feats += par[11:14]
        for c in range(NFEAT):
            stage[pl.ds(i * 128 + c, 8, stride=16), :] = feats[c]

    @pl.loop(0, blocks, unroll=8)
    def _(r):
        out_ref[r] = stage[pl.ds(pl.multiple_of(r * 16, 16), NFEAT), :]


def place(device):
    minor = lax.axis_size("cy")
    return (device // minor, lax.rem(device, minor))


def position():
    return lax.axis_index("cx") * lax.axis_size("cy") + lax.axis_index("cy")


def greet(peers):
    me = position()
    barrier = pltpu.get_barrier_semaphore()

    @pl.loop(1, peers)
    def _(off):
        pl.semaphore_signal(
            barrier,
            inc=1,
            device_id=place(lax.rem(me + off, peers)),
            device_id_type=pl.DeviceIdType.MESH,
        )

    pl.semaphore_wait(barrier, peers - 1)


def send(source, target, send_sem, recv_sem, peer):
    return pltpu.make_async_remote_copy(
        src_ref=source,
        dst_ref=target,
        send_sem=send_sem,
        recv_sem=recv_sem,
        device_id=place(peer),
        device_id_type=pl.DeviceIdType.MESH,
    )


def await_all(source, target, send_sem, recv_sem, peers):
    rest = send(
        source.at[pl.ds(0, peers - 1)],
        target.at[pl.ds(0, peers - 1)],
        send_sem,
        recv_sem,
        lax.rem(position() + 1, peers),
    )
    rest.wait_send()
    rest.wait_recv()


def invert(idx_ref, inv_ref, acc):
    steps, part = idx_ref.shape
    owners = inv_ref.shape[0]
    half = owners // 2
    hio = lax.broadcasted_iota(jnp.int32, (half, part), 0)
    loo = lax.broadcasted_iota(jnp.int32, (2 * LANES, part), 0)
    spot = lax.broadcasted_iota(jnp.int32, (1, part), 1)
    acc[...] = jnp.zeros_like(acc)

    @pl.loop(0, steps)
    def _(i):
        idx = idx_ref[pl.ds(i, 1), :]
        row = idx // LANES
        mine = hio == row % half
        high = (i * (part // LANES) + spot // LANES).astype(f32)
        low = (spot % LANES).astype(f32)
        left = jnp.concatenate(
            [jnp.where(mine, high, 0.0).astype(bf16), jnp.where(mine, low, 0.0).astype(bf16)], axis=0
        )
        lo = row // half * LANES + idx % LANES
        right = jnp.where(loo == lo, 1.0, 0.0).astype(bf16)
        acc[...] += lax.dot_general(left, right, NT_DIMS, preferred_element_type=f32)

    inv = acc[:half].astype(jnp.int32) * LANES + acc[half:].astype(jnp.int32)
    inv_ref[:half, :] = inv[:, :LANES]
    inv_ref[half:, :] = inv[:, LANES:]


def fetch_kernel(
    req_ref, params_ref, idx_ref,
    out_ref, asked_ref, inv_ref,
    asked_v, asked_s, table, stage, outgoing, acc, send1, recv1, send2, recv2, local,
):
    peers = out_ref.shape[0]
    me = position()
    greet(peers)

    @pl.loop(1, peers)
    def _(off):
        peer = lax.rem(me + off, peers)
        send(req_ref.at[peer], asked_v.at[me], send1, recv1, peer).start()

    asked_v[me] = req_ref[me]
    project(params_ref, table, stage)
    await_all(req_ref, asked_v, send1, recv1, peers)
    copy = pltpu.make_async_copy(asked_v, asked_s, local)
    copy.start()
    copy.wait()

    @pl.loop(1, peers)
    def _(off):
        peer = lax.rem(me + off, peers)
        outgoing[peer] = table[asked_s[peer, 0, 0]]
        send(outgoing.at[peer], out_ref.at[me], send2, recv2, peer).start()

    out_ref[me] = table[asked_s[me, 0, 0]]

    @pl.loop(0, peers)
    def _(d):
        asked_ref[d] = asked_s[d, 0, 0]

    invert(idx_ref, inv_ref, acc)
    await_all(outgoing, out_ref, send2, recv2, peers)


def return_kernel(
    grad_ref, inv_ref, out_ref, tabg, folded, outgoing, send_sem, recv_sem
):
    peers = out_ref.shape[0]
    me = position()
    steps = peers // 8
    greet(peers)
    fill_table(lambda c: grad_ref[c * LANES : (c + 1) * LANES, :], None, tabg, 0)

    @pl.loop(0, steps)
    def _(n):
        t = lax.rem(me // 8 + n, steps)
        idx = jnp.concatenate([inv_ref[pl.ds(t * 8 + q, 1), :] for q in range(8)], axis=1)
        rows = pick(idx, None, tabg, 0, folded)
        for c in range(NFEAT):
            outgoing[pl.ds(t * 8, 8), c, :] = rows[c]

        @pl.loop(0, 8)
        def _(q):
            peer = t * 8 + q

            @pl.when(peer != me)
            def _():
                send(outgoing.at[peer], out_ref.at[me], send_sem, recv_sem, peer).start()

    out_ref[me] = outgoing[me]
    await_all(outgoing, out_ref, send_sem, recv_sem, peers)


def unproject_kernel(params_ref, asked_ref, grad_ref, out_ref, stage):
    blocks = grad_ref.shape[0]
    stage_blocks(params_ref, asked_ref, stage, blocks)

    @pl.loop(0, blocks // 8)
    def _(i):
        par = [stage[pl.ds(i * 128 + c, 8, stride=16), :] for c in range(NPAR)]
        rows = pl.ds(pl.multiple_of(i * 8, 8), 8)
        grad = [grad_ref[rows, c, :] for c in range(NFEAT)]
        _, pull = jax.vjp(geometry, par[:10])
        res = list(pull(tuple(grad[:5]))[0])
        decay = jnp.exp(-par[10])
        res.append(grad[5] * (decay / (1.0 + decay)))
        res += grad[6:9]
        for c in range(NPAR):
            stage[pl.ds(i * 128 + c, 8, stride=16), :] = res[c]

    @pl.loop(0, blocks, unroll=8)
    def _(r):
        col = pl.multiple_of(asked_ref[r] * LANES, LANES)
        out_ref[:, pl.ds(col, LANES)] = stage[pl.ds(pl.multiple_of(r * 16, 16), NPAR), :]


def split(x, parts):
    out = []
    for _ in range(parts - 1):
        p = x.astype(bf16)
        out.append(p)
        x = x - p.astype(f32)
    out.append(x.astype(bf16))
    return out


def fill_table(read, table3, table2, deep):
    half = LANES // 2
    for c in range(NFEAT):
        xt = read(c).T
        n = 2 * xt.shape[1]
        rem = jnp.concatenate([xt[:half], xt[half:]], axis=1)
        for s, p in enumerate(split(rem, 3 if c < deep else 2)):
            if c < deep:
                table3[c * half : (c + 1) * half, s * n : (s + 1) * n] = p
            else:
                table2[(c - deep) * half : (c - deep + 1) * half, s * n : (s + 1) * n] = p


def pick(idx, table3, table2, deep, folded):
    half = LANES // 2
    n = idx.shape[1]
    rows = table2.shape[1] // 4
    kio = lax.broadcasted_iota(jnp.int32, (2 * rows, n), 0)
    lio = lax.broadcasted_iota(jnp.int32, (half, n), 0)
    hi = ((idx >> 6) & 1) * rows + (idx >> 7)
    mine = lio == (idx & (half - 1))
    oh = jnp.where(kio == hi, 1.0, 0.0).astype(bf16)
    if deep:
        t3 = jnp.dot(
            table3[...], jnp.concatenate([oh, oh, oh], axis=0), preferred_element_type=f32
        )
    t2 = jnp.dot(table2[...], jnp.concatenate([oh, oh], axis=0), preferred_element_type=f32)
    for c in range(NFEAT):
        if c < deep:
            v = t3[c * half : (c + 1) * half]
        else:
            v = t2[(c - deep) * half : (c - deep + 1) * half]
        v = jnp.where(mine, v, 0.0)
        part = v[0:8]
        for r in range(8, half, 8):
            part = part + v[r : r + 8]
        for q in range(n // LANES):
            folded[c * 64 + q * 8 : c * 64 + q * 8 + 8, :] = part[:, q * LANES : (q + 1) * LANES]
    out = []
    for c in range(NFEAT):
        total = folded[pl.ds(c * 64, 8, stride=8), :]
        for r in range(1, 8):
            total = total + folded[pl.ds(c * 64 + r, 8, stride=8), :]
        out.append(total)
    return out


PART = 1024
KC = 16
NB = 6
YS = [n + 0.5 for n in range(SIDE // 2)]


def swap_blocks(rows, lane):
    blk = lane // SIDE
    out = []
    for g in range(8):
        res = None
        for y in range(8):
            shift = ((y - g) * SIDE) % LANES
            r = pltpu.roll(rows[y], shift, 1) if shift else rows[y]
            res = r if res is None else jnp.where(blk == y, r, res)
        out.append(res)
    return out


def render_kernel(
    feat_ref, idx_ref, len_ref, off_ref, cot_ref, spread_ref, reduce_ref,
    img_ref, gsc_ref,
    tab3, tab2, folded, picked, stack, left, bcast, alpha, weight, trans, image, cots, moms, meta,
):
    steps = idx_ref.shape[0]
    fill_table(lambda c: feat_ref[:, c, :], tab3, tab2, 2)
    lane = lax.broadcasted_iota(jnp.int32, (8, LANES), 1)
    slot = lane % TG

    def per_tile(read):
        rows = []
        for g in range(8):
            row = jnp.full((1, LANES), read(g * TG), jnp.int32)
            for t in range(1, TG):
                row = jnp.where(slot[:1] == t, read(g * TG + t), row)
            rows.append(row)
        return jnp.concatenate(rows, axis=0)

    meta[0:8, :] = per_tile(lambda t: len_ref[t])
    meta[8:16, :] = per_tile(lambda t: off_ref[t, 0]) * SIDE + SIDE // 2
    meta[16:24, :] = per_tile(lambda t: off_ref[t, 1]) * SIDE + SIDE // 2
    stack[...] = jnp.zeros_like(stack)
    trans[...] = jnp.ones_like(trans)
    image[...] = jnp.zeros_like(image)
    for c in range(3):
        for h in range(2):
            rows = [cot_ref[pl.ds(g * 6 * TG + 2 * c + h, TG, stride=6), :] for g in range(8)]
            for y, val in enumerate(swap_blocks(rows, lane)):
                cots[(c * SIDE + h * 8 + y) * 8 : (c * SIDE + h * 8 + y + 1) * 8, :] = val

    def at_step(c, i):
        return pl.ds(pl.multiple_of(c * LANES + i * 8, 8), 8)

    @pl.loop(0, steps)
    def _(i):
        for c, val in enumerate(pick(idx_ref[pl.ds(i, 1), :], tab3, tab2, 2, folded)):
            picked[at_step(c, i), :] = val

    @pl.loop(0, steps)
    def _(i):
        f = [picked[at_step(c, i), :] for c in range(NFEAT)]
        live = (i * KC + lane // TG) < meta[0:8, :]
        u = f[0] - meta[8:16, :].astype(f32)
        v = f[1] - meta[16:24, :].astype(f32)
        a, b, c2 = f[2], f[3], f[4]
        picked[at_step(0, i), :] = u
        picked[at_step(1, i), :] = v
        pu = a * u + b * v
        pv = c2 * v + b * u
        k0 = f[5] - 0.5 * (u * pu + v * pv)
        vals = [
            jnp.where(live, LOG2E * k0, -1e30),
            jnp.where(live, LOG2E * pu, 0.0),
            jnp.where(live, LOG2E * pv, 0.0),
            jnp.where(live, (-0.5 * LOG2E) * a, 0.0),
            jnp.where(live, -LOG2E * b, 0.0),
            jnp.where(live, (-0.5 * LOG2E) * c2, 0.0),
            f[6],
            f[7],
            f[8],
        ]
        for n, val in enumerate(vals):
            for s, p in enumerate(split(val, 3)):
                at = s * 8 + n if n < 8 else 24 + s
                stack[pl.ds(at, 8, stride=32), :] = p.astype(f32)
        left[pl.ds(pl.multiple_of(i * LANES, LANES), LANES), :] = jnp.concatenate(
            [stack[:LANES].T, stack[LANES:].T], axis=1
        ).astype(bf16)

    bcast[...] = jnp.dot(left[...], spread_ref[...], preferred_element_type=f32)

    def forward(i):
        for hb in range(2):
            ys = list(range(4 * hb, 4 * hb + 4))
            spots = [(n, sg) for n in ys for sg in (1, -1)]
            yi = {(n, sg): (8 + n if sg > 0 else 7 - n) for n, sg in spots}
            tr = {p: trans[yi[p] * 8 : yi[p] * 8 + 8, :] for p in spots}
            im = {
                (c, p): image[(c * SIDE + yi[p]) * 8 : (c * SIDE + yi[p]) * 8 + 8, :]
                for p in spots
                for c in range(3)
            }
            for kl in range(KC):
                row = pl.ds(pl.multiple_of(i * (KC * 8) + kl * 8, 8), 8)
                pp, qq, rr, cr, cg, cb = [
                    bcast[row, n * LANES : (n + 1) * LANES] for n in range(NB)
                ]
                for n in ys:
                    even = pp + (YS[n] * YS[n]) * rr
                    odd = YS[n] * qq
                    for sg in (1, -1):
                        p = (n, sg)
                        e = jnp.exp2(even + odd if sg > 0 else even - odd)
                        al = jnp.minimum(e, 0.99)
                        w = al * tr[p]
                        tr[p] = tr[p] - w
                        at = pl.ds(pl.multiple_of((i * KC + kl) * PIX // 2 + yi[p] * 8, 8), 8)
                        alpha[at, :] = al
                        weight[at, :] = w
                        for c, col in enumerate((cr, cg, cb)):
                            im[c, p] = im[c, p] + col * w
            for p in spots:
                trans[yi[p] * 8 : yi[p] * 8 + 8, :] = tr[p]
                for c in range(3):
                    image[(c * SIDE + yi[p]) * 8 : (c * SIDE + yi[p]) * 8 + 8, :] = im[c, p]

    def backward(i):
        behind = {y: trans[y * 8 : y * 8 + 8, :] for y in range(SIDE)}
        for kl in reversed(range(KC)):
            row = pl.ds(pl.multiple_of(i * (KC * 8) + kl * 8, 8), 8)
            cols = [bcast[row, n * LANES : (n + 1) * LANES] for n in range(3, NB)]
            acc = [None] * NB

            def add(n, val):
                acc[n] = val if acc[n] is None else acc[n] + val

            for n in range(SIDE // 2):
                dq = {}
                for sg in (1, -1):
                    y = 8 + n if sg > 0 else 7 - n
                    at = pl.ds(pl.multiple_of((i * KC + kl) * PIX // 2 + y * 8, 8), 8)
                    al, w = alpha[at, :], weight[at, :]
                    ct = [cots[(c * SIDE + y) * 8 : (c * SIDE + y + 1) * 8, :] for c in range(3)]
                    d = cols[0] * ct[0] + cols[1] * ct[1] + cols[2] * ct[2] - behind[y]
                    behind[y] = behind[y] + al * d
                    dq[sg] = jnp.where(al < 0.99, w * d, 0.0)
                    for c in range(3):
                        add(3 + c, w * ct[c])
                both, diff = dq[1] + dq[-1], dq[1] - dq[-1]
                add(0, both)
                add(1, YS[n] * diff)
                add(2, (YS[n] * YS[n]) * both)
            for n in range(NB):
                bcast[row, n * LANES : (n + 1) * LANES] = acc[n]
        for y in range(SIDE):
            trans[y * 8 : y * 8 + 8, :] = behind[y]

    @pl.loop(0, steps)
    def _(i):
        forward(i)

    for c in range(3):
        for h in range(2):
            rows = [
                image[(c * SIDE + h * 8 + y) * 8 : (c * SIDE + h * 8 + y + 1) * 8, :]
                for y in range(8)
            ]
            for g, val in enumerate(swap_blocks(rows, lane)):
                img_ref[pl.ds(g * 6 * TG + 2 * c + h, TG, stride=6), :] = val

    trans[...] = jnp.zeros_like(trans)

    @pl.loop(0, steps)
    def _(n):
        backward(steps - 1 - n)

    batch = 4
    right = jnp.concatenate([reduce_ref[...]] * 3, axis=0)

    @pl.loop(0, steps // batch)
    def _(k):
        rows = pl.ds(pl.multiple_of(k * batch * LANES, LANES), batch * LANES)
        res = jnp.dot(
            jnp.concatenate(split(bcast[rows, :], 3), axis=1), right, preferred_element_type=f32
        )
        for q in range(batch):
            i = k * batch + q
            moms[q * LANES : (q + 1) * LANES, :] = res[q * LANES : (q + 1) * LANES].T
            m = [moms[pl.ds(q * LANES + n, 8, stride=16), :] for n in range(NFEAT)]
            u, v, a, b, c2 = [picked[at_step(n, i), :] for n in range(5)]
            s0, sx, sy, sxx, sxy, syy = m[:6]
            mx = sx - u * s0
            my = sy - v * s0
            out = [
                a * mx + b * my,
                c2 * my + b * mx,
                -0.5 * (sxx - u * (sx + mx)),
                -(sxy - u * sy - v * mx),
                -0.5 * (syy - v * (sy + my)),
                s0,
            ] + m[6:]
            for c in range(NFEAT):
                gsc_ref[at_step(c, i), :] = out[c]


def constants():
    x = np.arange(SIDE) - (SIDE - 1) / 2.0
    one = np.ones(SIDE)
    spread = np.zeros((8, 32, NB, 8, SIDE), np.float32)
    reduce = np.zeros((NB, 8, SIDE, 8, 16), np.float32)
    for g in range(8):
        for s in range(3):
            for row, q, val in (
                (0, 0, one), (1, 0, x), (3, 0, x * x), (2, 1, one), (4, 1, x), (5, 2, one),
                (6, 3, one), (7, 4, one),
            ):
                spread[g, s * 8 + row, q, g] = val
            spread[g, 24 + s, 5, g] = one
        for q, m, val in (
            (0, 0, one), (0, 1, x), (0, 3, x * x), (1, 2, one), (1, 4, x), (2, 5, one),
            (3, 6, one), (4, 7, one), (5, 8, one),
        ):
            reduce[q, g, :, g, m] = val
    return (
        jnp.asarray(spread.reshape(256, NB * LANES), bf16),
        jnp.asarray(reduce.reshape(NB * LANES, LANES), bf16),
    )


VM = pl.BlockSpec(memory_space=pltpu.VMEM)
SM = pl.BlockSpec(memory_space=pltpu.SMEM)
LIMIT = pltpu.CompilerParams(vmem_limit_bytes=56 * 1024 * 1024)


REMOTE = dict(has_side_effects=True, vmem_limit_bytes=40 * 1024 * 1024)


def fetch(requests, params, idx):
    peers = requests.shape[1]
    wanted = jnp.broadcast_to(requests.reshape(peers, 1, 1), (peers, 1, LANES))
    return pl.pallas_call(
        fetch_kernel,
        out_shape=(
            jax.ShapeDtypeStruct((peers, NFEAT, LANES), f32),
            jax.ShapeDtypeStruct((peers,), jnp.int32),
            jax.ShapeDtypeStruct((peers, LANES), jnp.int32),
        ),
        in_specs=[VM, VM, VM],
        out_specs=(VM, SM, VM),
        scratch_shapes=[
            pltpu.VMEM((peers, 1, LANES), jnp.int32),
            pltpu.SMEM((peers, 1, LANES), jnp.int32),
            pltpu.VMEM((peers, NFEAT, LANES), f32),
            pltpu.VMEM((peers * 16, LANES), f32),
            pltpu.VMEM((peers, NFEAT, LANES), f32),
            pltpu.VMEM((peers, 2 * LANES), f32),
        ]
        + [pltpu.SemaphoreType.DMA] * 5,
        compiler_params=pltpu.CompilerParams(collective_id=0, **REMOTE),
        name="fetch",
    )(wanted, params, idx)


def give_back(grads, inv):
    peers = inv.shape[0]
    return pl.pallas_call(
        return_kernel,
        out_shape=jax.ShapeDtypeStruct((peers, NFEAT, LANES), f32),
        in_specs=[VM, VM],
        out_specs=VM,
        scratch_shapes=[
            pltpu.VMEM((NFEAT * LANES // 2, 4 * LANES), bf16),
            pltpu.VMEM((NFEAT * 64, LANES), f32),
            pltpu.VMEM((peers, NFEAT, LANES), f32),
        ]
        + [pltpu.SemaphoreType.DMA] * 2,
        compiler_params=pltpu.CompilerParams(collective_id=1, **REMOTE),
        name="give_back",
    )(grads, inv)


def per_device(params, requests, lists, list_len, offsets, cotangent):
    peers = lax.axis_size(AXES)
    g_dev = params.shape[1]
    tiles, length = lists.shape
    steps = length // KC
    idx = lists.reshape(8, TG, steps, KC).transpose(2, 0, 3, 1).reshape(steps, PART)
    fetched, asked, inv = fetch(requests, params, idx)
    spread, reduce = constants()
    image, gfeat = pl.pallas_call(
        render_kernel,
        out_shape=(
            jax.ShapeDtypeStruct((tiles * 6, LANES), f32),
            jax.ShapeDtypeStruct((NFEAT * LANES, LANES), f32),
        ),
        in_specs=[VM, VM, SM, SM, VM, VM, VM],
        out_specs=(VM, VM),
        scratch_shapes=[
            pltpu.VMEM((LANES, 6 * peers), bf16),
            pltpu.VMEM((7 * LANES // 2, 4 * peers), bf16),
            pltpu.VMEM((NFEAT * 64, LANES), f32),
            pltpu.VMEM((NFEAT * LANES, LANES), f32),
            pltpu.VMEM((256, LANES), f32),
            pltpu.VMEM((length * 8, 256), bf16),
            pltpu.VMEM((length * 8, NB * LANES), f32),
            pltpu.VMEM((length * SIDE * 8, LANES), f32),
            pltpu.VMEM((length * SIDE * 8, LANES), f32),
            pltpu.VMEM((SIDE * 8, LANES), f32),
            pltpu.VMEM((3 * SIDE * 8, LANES), f32),
            pltpu.VMEM((3 * SIDE * 8, LANES), f32),
            pltpu.VMEM((4 * LANES, LANES), f32),
            pltpu.VMEM((24, LANES), jnp.int32),
        ],
        compiler_params=LIMIT,
        name="render",
    )(
        fetched,
        idx,
        list_len,
        offsets,
        cotangent.reshape(tiles * 6, LANES),
        spread,
        reduce,
    )

    landed = give_back(gfeat, inv)
    grads = pl.pallas_call(
        unproject_kernel,
        out_shape=jax.ShapeDtypeStruct((NPAR, g_dev), f32),
        in_specs=[VM, SM, VM],
        out_specs=VM,
        scratch_shapes=[pltpu.VMEM((peers * 16, LANES), f32)],
        compiler_params=LIMIT,
        name="unproject",
    )(params, asked, landed)
    return image.reshape(tiles, 3, PIX), grads


def solution(mesh):
    in_specs = (
        P(None, AXES),
        P(AXES, None, None),
        P(AXES, None),
        P(AXES),
        P(AXES, None),
        P(AXES, None, None),
    )
    out_specs = (P(AXES, None, None), P(None, AXES))
    return jax.shard_map(
        per_device, mesh=mesh, in_specs=in_specs, out_specs=out_specs, check_vma=False
    )
```

time: 580 us -> 118 us (0.20); the launches traced: 572 us -> 118 us
  other arithmetic: 198 us -> 0 us
  local copies, waits for them, and re-layouts: 188 us -> 8.96 us
  matrix products: 118 us -> 0 us
  Pallas kernels: 0 us -> 108 us
  waiting for transfers between devices: 25.6 us -> 0 us
  blocking collectives: 23 us -> 0 us
  starting transfers between devices: 15.8 us -> 0 us
    dot_general x21 -> x0, matrix products: 118 us -> none  [the longest x12 61.3 us: tile_image(): jnp.einsum('ck,pk->cp', features[6:9], weight, precision=lax.Precision.HI...]
    pallas_call x0 -> x4, Pallas kernels: none -> 108 us  [the longest x1 46.6 us: per_device(): pl.pallas_call(render_kernel, out_shape=(jax.ShapeDtypeStruct((tiles * 6,...]
    scatter-add x1 -> x0, other arithmetic: 91.4 us -> none  [per_device(): jnp.zeros((9, feats.shape[1]), jnp.float32).at[:, lists.reshape(-1)]]
    another operation x2 -> x0, local copies, waits for them, and re-layouts: 60.5 us -> none  [project(): jnp.stack([focal * xpos / depth, focal * ypos / depth, cov_c / determ, -c...]
    gather x9 -> x0, local copies, waits for them, and re-layouts: 59.8 us -> none  [the longest x8 59.1 us: per_tile(): gathered = jnp.take(feats, entries, axis=1)]
    reduce_sum x8 -> x0, other arithmetic: 54.8 us -> none  [the longest x4 37.2 us: tile_image(): features[3] * delta_x * delta_y]
    unnamed x137 -> x21, local copies, waits for them, and re-layouts: 59.3 us -> 6.33 us
    mul x15 -> x0, other arithmetic: 28 us -> none  [the longest x4 23.6 us: tile_image(): alpha = jnp.minimum(0.99, features[5] * jnp.exp(power)) * live[None, :]]
  transfers between devices with their start and end apart: 2 -> 0, of which waited for: 2 -> 0; matrix products, arithmetic and copies ran while one was open for 1% -> 0% of each run, Pallas kernels for 0% -> 0%
where the time goes in v2:
time: 118 us
  Pallas kernels  108 us (92%)
  local copies, waits for them, and re-layouts  8.96 us (8%)
    pallas_call x1, Pallas kernels, per_device(): pl.pallas_call(render_kernel, out_shape=(jax.ShapeDtypeStruct((tiles * 6,...  46.6 us
    pallas_call x1, Pallas kernels, fetch(): pl.pallas_call(fetch_kernel, out_shape=(jax.ShapeDtypeStruct((peers, NFEA...  30.3 us
    pallas_call x1, Pallas kernels, give_back(): pl.pallas_call(return_kernel, out_shape=jax.ShapeDtypeStruct((peers, NFEA...  26.4 us
    unnamed x21, local copies, waits for them, and re-layouts  6.33 us
    pallas_call x1, Pallas kernels, per_device(): pl.pallas_call(unproject_kernel, out_shape=jax.ShapeDtypeStruct((NPAR, g_...  5 us

profile of v2, /device:TPU:1, one launch (start us, length us, event | category | flops | bytes accessed | tf_op | source)
XLA Modules:
  0.0 118.0 jit_solution(3390599892523449921)
XLA Ops:
  0.6 0.0 copy-start.7
  0.6 0.7 copy-done.7
  1.3 0.0 copy-start.8
  1.3 0.7 copy.18.off_ref
  2.0 0.0 copy-done.8
  2.0 0.2 broadcast_in_dim.8.req_ref
  2.2 1.1 copy.16
  3.3 0.0 copy-start.6
  3.3 0.8 reshape.22.cot_ref
  4.1 0.0 copy-done.6
  4.1 0.0 copy-start
  4.1 0.2 reshape.20
  4.3 0.2 copy.14
  4.5 0.2 copy.15.idx_ref
  4.7 0.6 copy-done
  5.4 0.0 copy-start.3
  5.4 30.3 %fetch.1 = (f32[128,9,128]{2,1,0:T(8,128)S(1)}, s32[128]{0:T(128)S(1)}, s32[128,128]{1,0:T(8,128)S(1)}) custom-call(s32[128,1,128]{2,1,0:T(1,128)S(1)} %broadcast_in_dim.8.req_ref, f32[14,16384]{1,0:T(8,128)S(1)} %copy-done, s32[16,1024]{1,0:T(8,128)S(1)} %copy.15.idx_ref), custom_call_target="tpu_custom_call" | custom-call | tf_op jit(solution)/shard_map/fetch/pallas_call | solution.py:557
  35.6 0.0 copy-done.3
  35.6 0.0 copy-start.2
  35.6 1.0 copy-done.2
  36.6 0.0 copy-start.5
  36.6 0.5 copy-done.5
  37.1 46.6 %render.1 = (f32[384,128]{1,0:T(8,128)}, f32[1152,128]{1,0:T(8,128)}) custom-call(f32[128,9,128]{2,1,0:T(8,128)} %copy-done.2, s32[16,1024]{1,0:T(8,128)} %copy-done.3, s32[64]{0:T(128)} %len_ref.1, s32[64,2]{1,0:T(8,128)} %copy.18.off_ref, f32[384,128]{1,0:T(8,128)} %reshape.22.cot_ref, bf16[256,768]{1,0:T(8,128)(2,1)} %constant.4.clone.spread_ref, ...), custom_call_target="tpu_custom_call" | custom-call | tf_op jit(solution)/shard_map/render/pallas_call | solution.py:606
  83.8 0.0 copy-start.4
  83.8 1.1 reshape.23
  84.9 0.7 copy.19
  85.6 0.0 copy-done.4
  85.6 26.4 %give_back.1.grad_ref = f32[128,9,128]{2,1,0:T(8,128)S(1)} custom-call(f32[1152,128]{1,0:T(8,128)S(1)} %copy-done.4, s32[128,128]{1,0:T(8,128)S(1)} %get-tuple-element.11.inv_ref), custom_call_target="tpu_custom_call" | custom-call | tf_op jit(solution)/shard_map/give_back/pallas_call | solution.py:582
  112.0 0.0 copy-start.1
  112.0 1.0 copy-done.1
  113.0 5.0 %unproject.1 = f32[14,16384]{1,0:T(8,128)} custom-call(f32[14,16384]{1,0:T(8,128)} %params_ref.3, s32[128]{0:T(128)} %copy-done.5, f32[128,9,128]{2,1,0:T(8,128)} %copy-done.1), custom_call_target="tpu_custom_call" | custom-call | tf_op jit(solution)/shard_map/unproject/pallas_call | solution.py:643
Async XLA Ops:
  0.6 0.7 copy-start.7
  1.3 0.7 copy-start.8
  3.3 0.8 copy-start.6
  4.1 1.2 %copy-start = (f32[14,16384]{1,0:T(8,128)S(1)}, f32[14,16384]{1,0:T(8,128)}, u32[]{:S(2)}) copy-start(f32[14,16384]{1,0:T(8,128)} %params_ref.3) | copy-start | bytes 2752516
  5.4 30.3 %copy-start.3 = (s32[16,1024]{1,0:T(8,128)}, s32[16,1024]{1,0:T(8,128)S(1)}, u32[]{:S(2)}) copy-start(s32[16,1024]{1,0:T(8,128)S(1)} %copy.15.idx_ref) | copy-start | bytes 196612
  35.6 1.0 copy-start.2
  36.6 0.5 copy-start.5
  83.8 1.8 %copy-start.4 = (f32[1152,128]{1,0:T(8,128)S(1)}, f32[1152,128]{1,0:T(8,128)}, u32[]{:S(2)}) copy-start(f32[1152,128]{1,0:T(8,128)} %get-tuple-element.10.grad_ref) | copy-start | bytes 1769476
  112.0 1.0 copy-start.1

commit v3 on v2

--- a/solution.py
+++ b/solution.py
@@ -114,7 +114,9 @@
             device_id_type=pl.DeviceIdType.MESH,
         )
 
-    pl.semaphore_wait(barrier, peers - 1)
+
+def hear(peers):
+    pl.semaphore_wait(pltpu.get_barrier_semaphore(), peers - 1)
 
 
 def send(source, target, send_sem, recv_sem, peer):
@@ -141,7 +143,7 @@
 
 
 def invert(idx_ref, inv_ref, acc):
-    steps, part = idx_ref.shape
+    steps, part = idx_ref.shape[0] // 8, PART
     owners = inv_ref.shape[0]
     half = owners // 2
     hio = lax.broadcasted_iota(jnp.int32, (half, part), 0)
@@ -151,7 +153,8 @@
 
     @pl.loop(0, steps)
     def _(i):
-        idx = idx_ref[pl.ds(i, 1), :]
+        idx8 = idx_ref[rows8(i), :]
+        idx = jnp.concatenate([idx8[q : q + 1] for q in range(8)], axis=1)
         row = idx // LANES
         mine = hio == row % half
         high = (i * (part // LANES) + spot // LANES).astype(f32)
@@ -176,6 +179,8 @@
     peers = out_ref.shape[0]
     me = position()
     greet(peers)
+    project(params_ref, table, stage)
+    hear(peers)
 
     @pl.loop(1, peers)
     def _(off):
@@ -183,7 +188,6 @@
         send(req_ref.at[peer], asked_v.at[me], send1, recv1, peer).start()
 
     asked_v[me] = req_ref[me]
-    project(params_ref, table, stage)
     await_all(req_ref, asked_v, send1, recv1, peers)
     copy = pltpu.make_async_copy(asked_v, asked_s, local)
     copy.start()
@@ -206,29 +210,38 @@
 
 
 def return_kernel(
-    grad_ref, inv_ref, out_ref, tabg, folded, outgoing, send_sem, recv_sem
+    grad_ref, inv_ref, out_ref, table, folded, outgoing, send_sem, recv_sem
 ):
     peers = out_ref.shape[0]
     me = position()
     steps = peers // 8
     greet(peers)
-    fill_table(lambda c: grad_ref[c * LANES : (c + 1) * LANES, :], None, tabg, 0)
-
-    @pl.loop(0, steps)
+    fill_table(lambda c: grad_ref[c * LANES : (c + 1) * LANES, :], table, EXACT_BACK)
+    hear(peers)
+
+    @pl.loop(1, steps + 1)
     def _(n):
         t = lax.rem(me // 8 + n, steps)
-        idx = jnp.concatenate([inv_ref[pl.ds(t * 8 + q, 1), :] for q in range(8)], axis=1)
-        rows = pick(idx, None, tabg, 0, folded)
+        rows = pick(
+            inv_ref[rows8(t), :], table, EXACT_BACK, folded,
+            lambda c, h: grad_ref[c * LANES + h : c * LANES + h + 1, :],
+        )
         for c in range(NFEAT):
             outgoing[pl.ds(t * 8, 8), c, :] = rows[c]
 
-        @pl.loop(0, 8)
-        def _(q):
-            peer = t * 8 + q
-
-            @pl.when(peer != me)
-            def _():
+        @pl.when(n < steps)
+        def _():
+            for q in range(8):
+                peer = t * 8 + q
                 send(outgoing.at[peer], out_ref.at[me], send_sem, recv_sem, peer).start()
+
+    @pl.loop(0, 8)
+    def _(q):
+        peer = me // 8 * 8 + q
+
+        @pl.when(peer != me)
+        def _():
+            send(outgoing.at[peer], out_ref.at[me], send_sem, recv_sem, peer).start()
 
     out_ref[me] = outgoing[me]
     await_all(outgoing, out_ref, send_sem, recv_sem, peers)
@@ -267,46 +280,49 @@
     return out
 
 
-def fill_table(read, table3, table2, deep):
+def fill_table(read, table, first):
     half = LANES // 2
-    for c in range(NFEAT):
+    for c in range(first, NFEAT):
         xt = read(c).T
         n = 2 * xt.shape[1]
         rem = jnp.concatenate([xt[:half], xt[half:]], axis=1)
-        for s, p in enumerate(split(rem, 3 if c < deep else 2)):
-            if c < deep:
-                table3[c * half : (c + 1) * half, s * n : (s + 1) * n] = p
-            else:
-                table2[(c - deep) * half : (c - deep + 1) * half, s * n : (s + 1) * n] = p
-
-
-def pick(idx, table3, table2, deep, folded):
+        for s, p in enumerate(split(rem, 2)):
+            table[(c - first) * half : (c - first + 1) * half, s * n : (s + 1) * n] = p
+
+
+def rows8(i):
+    return pl.ds(pl.multiple_of(i * 8, 8), 8)
+
+
+def pick(idx8, table, first, folded, row):
     half = LANES // 2
+    idx = jnp.concatenate([idx8[q : q + 1] for q in range(8)], axis=1)
     n = idx.shape[1]
-    rows = table2.shape[1] // 4
+    rows = table.shape[1] // 4
     kio = lax.broadcasted_iota(jnp.int32, (2 * rows, n), 0)
     lio = lax.broadcasted_iota(jnp.int32, (half, n), 0)
     hi = ((idx >> 6) & 1) * rows + (idx >> 7)
     mine = lio == (idx & (half - 1))
     oh = jnp.where(kio == hi, 1.0, 0.0).astype(bf16)
-    if deep:
-        t3 = jnp.dot(
-            table3[...], jnp.concatenate([oh, oh, oh], axis=0), preferred_element_type=f32
-        )
-    t2 = jnp.dot(table2[...], jnp.concatenate([oh, oh], axis=0), preferred_element_type=f32)
-    for c in range(NFEAT):
-        if c < deep:
-            v = t3[c * half : (c + 1) * half]
-        else:
-            v = t2[(c - deep) * half : (c - deep + 1) * half]
-        v = jnp.where(mine, v, 0.0)
+    t2 = jnp.dot(table[...], jnp.concatenate([oh, oh], axis=0), preferred_element_type=f32)
+    hi8, lo8 = idx8 >> 7, idx8 & (LANES - 1)
+    exact = [jnp.zeros((8, LANES), f32)] * first
+    for h in range(rows):
+        here = hi8 == h
+        for c in range(first):
+            val = jnp.take_along_axis(
+                jnp.broadcast_to(row(c, h), (8, LANES)), lo8, axis=1, mode="promise_in_bounds"
+            )
+            exact[c] = jnp.where(here, val, exact[c])
+    for c in range(first, NFEAT):
+        v = jnp.where(mine, t2[(c - first) * half : (c - first + 1) * half], 0.0)
         part = v[0:8]
         for r in range(8, half, 8):
             part = part + v[r : r + 8]
         for q in range(n // LANES):
             folded[c * 64 + q * 8 : c * 64 + q * 8 + 8, :] = part[:, q * LANES : (q + 1) * LANES]
-    out = []
-    for c in range(NFEAT):
+    out = list(exact)
+    for c in range(first, NFEAT):
         total = folded[pl.ds(c * 64, 8, stride=8), :]
         for r in range(1, 8):
             total = total + folded[pl.ds(c * 64 + r, 8, stride=8), :]
@@ -314,6 +330,8 @@
     return out
 
 
+EXACT = 3
+EXACT_BACK = 3
 PART = 1024
 KC = 16
 NB = 6
@@ -336,10 +354,10 @@
 def render_kernel(
     feat_ref, idx_ref, len_ref, off_ref, cot_ref, spread_ref, reduce_ref,
     img_ref, gsc_ref,
-    tab3, tab2, folded, picked, stack, left, bcast, alpha, weight, trans, image, cots, moms, meta,
+    table, folded, picked, stack, left, bcast, alpha, weight, trans, image, cots, moms, meta,
 ):
-    steps = idx_ref.shape[0]
-    fill_table(lambda c: feat_ref[:, c, :], tab3, tab2, 2)
+    steps = idx_ref.shape[0] // 8
+    fill_table(lambda c: feat_ref[:, c, :], table, EXACT)
     lane = lax.broadcasted_iota(jnp.int32, (8, LANES), 1)
     slot = lane % TG
 
@@ -353,14 +371,14 @@
         return jnp.concatenate(rows, axis=0)
 
     meta[0:8, :] = per_tile(lambda t: len_ref[t])
-    meta[8:16, :] = per_tile(lambda t: off_ref[t, 0]) * SIDE + SIDE // 2
-    meta[16:24, :] = per_tile(lambda t: off_ref[t, 1]) * SIDE + SIDE // 2
+    meta[8:16, :] = per_tile(lambda t: off_ref[0, t]) * SIDE + SIDE // 2
+    meta[16:24, :] = per_tile(lambda t: off_ref[1, t]) * SIDE + SIDE // 2
     stack[...] = jnp.zeros_like(stack)
     trans[...] = jnp.ones_like(trans)
     image[...] = jnp.zeros_like(image)
     for c in range(3):
         for h in range(2):
-            rows = [cot_ref[pl.ds(g * 6 * TG + 2 * c + h, TG, stride=6), :] for g in range(8)]
+            rows = [cot_ref[c, g * TG : (g + 1) * TG, h * LANES : (h + 1) * LANES] for g in range(8)]
             for y, val in enumerate(swap_blocks(rows, lane)):
                 cots[(c * SIDE + h * 8 + y) * 8 : (c * SIDE + h * 8 + y + 1) * 8, :] = val
 
@@ -369,7 +387,9 @@
 
     @pl.loop(0, steps)
     def _(i):
-        for c, val in enumerate(pick(idx_ref[pl.ds(i, 1), :], tab3, tab2, 2, folded)):
+        for c, val in enumerate(
+            pick(idx_ref[rows8(i), :], table, EXACT, folded, lambda c, h: feat_ref[h, c : c + 1, :])
+        ):
             picked[at_step(c, i), :] = val
 
     @pl.loop(0, steps)
@@ -482,7 +502,7 @@
                 for y in range(8)
             ]
             for g, val in enumerate(swap_blocks(rows, lane)):
-                img_ref[pl.ds(g * 6 * TG + 2 * c + h, TG, stride=6), :] = val
+                img_ref[c, g * TG : (g + 1) * TG, h * LANES : (h + 1) * LANES] = val
 
     trans[...] = jnp.zeros_like(trans)
 
@@ -545,7 +565,7 @@
 
 VM = pl.BlockSpec(memory_space=pltpu.VMEM)
 SM = pl.BlockSpec(memory_space=pltpu.SMEM)
-LIMIT = pltpu.CompilerParams(vmem_limit_bytes=56 * 1024 * 1024)
+LIMIT = pltpu.CompilerParams(vmem_limit_bytes=50 * 1024 * 1024)
 
 
 REMOTE = dict(has_side_effects=True, vmem_limit_bytes=40 * 1024 * 1024)
@@ -585,7 +605,7 @@
         in_specs=[VM, VM],
         out_specs=VM,
         scratch_shapes=[
-            pltpu.VMEM((NFEAT * LANES // 2, 4 * LANES), bf16),
+            pltpu.VMEM(((NFEAT - EXACT_BACK) * LANES // 2, 4 * LANES), bf16),
             pltpu.VMEM((NFEAT * 64, LANES), f32),
             pltpu.VMEM((peers, NFEAT, LANES), f32),
         ]
@@ -600,20 +620,19 @@
     g_dev = params.shape[1]
     tiles, length = lists.shape
     steps = length // KC
-    idx = lists.reshape(8, TG, steps, KC).transpose(2, 0, 3, 1).reshape(steps, PART)
+    idx = lists.reshape(8, TG, steps, KC).transpose(2, 0, 3, 1).reshape(steps * 8, LANES)
     fetched, asked, inv = fetch(requests, params, idx)
     spread, reduce = constants()
     image, gfeat = pl.pallas_call(
         render_kernel,
         out_shape=(
-            jax.ShapeDtypeStruct((tiles * 6, LANES), f32),
+            jax.ShapeDtypeStruct((3, tiles, PIX), f32),
             jax.ShapeDtypeStruct((NFEAT * LANES, LANES), f32),
         ),
         in_specs=[VM, VM, SM, SM, VM, VM, VM],
         out_specs=(VM, VM),
         scratch_shapes=[
-            pltpu.VMEM((LANES, 6 * peers), bf16),
-            pltpu.VMEM((7 * LANES // 2, 4 * peers), bf16),
+            pltpu.VMEM(((NFEAT - EXACT) * LANES // 2, 4 * peers), bf16),
             pltpu.VMEM((NFEAT * 64, LANES), f32),
             pltpu.VMEM((NFEAT * LANES, LANES), f32),
             pltpu.VMEM((256, LANES), f32),
@@ -633,8 +652,8 @@
         fetched,
         idx,
         list_len,
-        offsets,
-        cotangent.reshape(tiles * 6, LANES),
+        offsets.T,
+        cotangent.transpose(1, 0, 2),
         spread,
         reduce,
     )
@@ -646,10 +665,10 @@
         in_specs=[VM, SM, VM],
         out_specs=VM,
         scratch_shapes=[pltpu.VMEM((peers * 16, LANES), f32)],
-        compiler_params=LIMIT,
+        compiler_params=pltpu.CompilerParams(vmem_limit_bytes=16 * 1024 * 1024),
         name="unproject",
     )(params, asked, landed)
-    return image.reshape(tiles, 3, PIX), grads
+    return image.transpose(1, 0, 2), grads
 
 
 def solution(mesh):

time: 118 us -> 102 us (0.86)
  Pallas kernels: 108 us -> 98.3 us
  local copies, waits for them, and re-layouts: 8.96 us -> 2.93 us
    unnamed x21 -> x14, local copies, waits for them, and re-layouts: 6.33 us -> 0.98 us
    pallas_call x1, Pallas kernels: 46.6 us -> 41.4 us  [per_device(): pl.pallas_call(render_kernel, out_shape=(jax.ShapeDtypeStruct((3, tiles,...]
    pallas_call x1, Pallas kernels: 26.4 us -> 22.5 us  [give_back(): pl.pallas_call(return_kernel, out_shape=jax.ShapeDtypeStruct((peers, NFEA...]
    reshape x5 -> x3, local copies, waits for them, and re-layouts: 2.44 us -> 1.07 us  [per_device(): lists.reshape(8, TG, steps, KC).transpose(2, 0, 3, 1)]
where the time goes in v3:
time: 102 us
  Pallas kernels  98.3 us (96%)
  local copies, waits for them, and re-layouts  2.93 us (3%)
    pallas_call x1, Pallas kernels, per_device(): pl.pallas_call(render_kernel, out_shape=(jax.ShapeDtypeStruct((3, tiles,...  41.4 us
    pallas_call x1, Pallas kernels, fetch(): pl.pallas_call(fetch_kernel, out_shape=(jax.ShapeDtypeStruct((peers, NFEA...  30.4 us
    pallas_call x1, Pallas kernels, give_back(): pl.pallas_call(return_kernel, out_shape=jax.ShapeDtypeStruct((peers, NFEA...  22.5 us
    pallas_call x1, Pallas kernels, per_device(): pl.pallas_call(unproject_kernel, out_shape=jax.ShapeDtypeStruct((NPAR, g_...  4 us

profile of v3, /device:TPU:1, one launch (start us, length us, event | category | flops | bytes accessed | tf_op | source)
XLA Modules:
  0.0 102.0 jit_solution(12698048727293442429)
XLA Ops:
  0.6 0.0 copy-start.6
  0.6 0.9 broadcast_in_dim.8.req_ref
  1.5 0.0 copy-done.6
  1.5 0.2 reshape.14
  1.7 0.0 copy-start
  1.7 0.4 copy.11
  2.1 0.5 reshape.15.idx_ref
  2.6 0.3 copy-done
  3.0 0.0 copy-start.1
  3.0 0.0 copy-start.2
  3.0 0.0 copy-start.3
  3.0 30.4 %fetch.1 = (f32[128,9,128]{2,1,0:T(8,128)S(1)}, s32[128]{0:T(128)S(1)}, s32[128,128]{1,0:T(8,128)S(1)}) custom-call(s32[128,1,128]{2,1,0:T(1,128)S(1)} %broadcast_in_dim.8.req_ref, f32[14,16384]{1,0:T(8,128)S(1)} %copy-done, s32[128,128]{1,0:T(8,128)S(1)} %reshape.15.idx_ref), custom_call_target="tpu_custom_call" | custom-call | tf_op jit(solution)/shard_map/fetch/pallas_call | solution.py:577
  33.4 0.0 copy-start.4
  33.4 0.0 copy-start.5
  33.4 0.0 copy-done.1
  33.4 0.0 copy-done.2
  33.4 0.0 copy-done.3
  33.5 0.6 copy-done.4
  34.1 0.0 copy-done.5
  34.1 41.4 %render.1 = (f32[3,64,256]{2,1,0:T(8,128)}, f32[1152,128]{1,0:T(8,128)S(1)}) custom-call(f32[128,9,128]{2,1,0:T(8,128)S(1)} %get-tuple-element.7.feat_ref, s32[128,128]{1,0:T(8,128)S(1)} %reshape.15.idx_ref, s32[64]{0:T(128)S(1)} %copy-done.5, s32[2,64]{1,0:T(2,128)S(1)} %bitcast.8, f32[3,64,256]{2,1,0:T(8,128)S(1)} %bitcast.7, ...), custom_call_target="tpu_custom_call" | custom-call | tf_op jit(solution)/shard_map/render/pallas_call | solution.py:626
  75.5 22.5 %give_back.1.grad_ref = f32[128,9,128]{2,1,0:T(8,128)S(1)} custom-call(f32[1152,128]{1,0:T(8,128)S(1)} %get-tuple-element.10.grad_ref, s32[128,128]{1,0:T(8,128)S(1)} %get-tuple-element.11.inv_ref), custom_call_target="tpu_custom_call" | custom-call | tf_op jit(solution)/shard_map/give_back/pallas_call | solution.py:602
  98.0 4.0 %unproject.1 = f32[14,16384]{1,0:T(8,128)} custom-call(f32[14,16384]{1,0:T(8,128)S(1)} %copy-done, s32[128]{0:T(128)S(1)} %get-tuple-element.9.asked_ref, f32[128,9,128]{2,1,0:T(8,128)S(1)} %give_back.1.grad_ref), custom_call_target="tpu_custom_call" | custom-call | tf_op jit(solution)/shard_map/unproject/pallas_call | solution.py:662
Async XLA Ops:
  0.6 0.9 copy-start.6
  1.7 1.2 %copy-start = (f32[14,16384]{1,0:T(8,128)S(1)}, f32[14,16384]{1,0:T(8,128)}, u32[]{:S(2)}) copy-start(f32[14,16384]{1,0:T(8,128)} %params_ref.3) | copy-start | bytes 2752516
  3.0 30.5 %copy-start.1 = (bf16[256,768]{1,0:T(8,128)(2,1)S(1)}, bf16[256,768]{1,0:T(8,128)(2,1)}, u32[]{:S(2)}) copy-start(bf16[256,768]{1,0:T(8,128)(2,1)} %constant.4.clone.spread_ref) | copy-start | bytes 1179652
  3.0 30.5 %copy-start.2 = (f32[64,3,256]{2,0,1:T(8,128)S(1)}, f32[64,3,256]{2,0,1:T(8,128)}, u32[]{:S(2)}) copy-start(f32[64,3,256]{2,0,1:T(8,128)} %param.13) | copy-start | bytes 589828
  3.0 30.5 %copy-start.3 = (bf16[768,128]{1,0:T(8,128)(2,1)S(1)}, bf16[768,128]{1,0:T(8,128)(2,1)}, u32[]{:S(2)}) copy-start(bf16[768,128]{1,0:T(8,128)(2,1)} %constant.5.clone.reduce_ref) | copy-start | bytes 589828
  33.4 0.7 copy-start.4
  33.4 0.7 copy-start.5

commit v4 on v3

--- a/solution.py
+++ b/solution.py
@@ -92,54 +92,59 @@
         out_ref[r] = stage[pl.ds(pl.multiple_of(r * 16, 16), NFEAT), :]
 
 
-def place(device):
-    minor = lax.axis_size("cy")
-    return (device // minor, lax.rem(device, minor))
-
-
 def position():
     return lax.axis_index("cx") * lax.axis_size("cy") + lax.axis_index("cy")
 
 
-def greet(peers):
-    me = position()
+def wrap(value, size):
+    return jnp.where(value >= size, value - size, value)
+
+
+def around(body):
+    nx, ny = lax.axis_size("cx"), lax.axis_size("cy")
+    cx, cy = lax.axis_index("cx"), lax.axis_index("cy")
+
+    def line(x, first):
+        @pl.loop(first, ny)
+        def _(dy):
+            y = wrap(cy + dy, ny)
+            body(x * ny + y, (x, y))
+
+    line(cx, 1)
+
+    @pl.loop(1, nx)
+    def _(dx):
+        line(wrap(cx + dx, nx), 0)
+
+
+def greet():
     barrier = pltpu.get_barrier_semaphore()
 
-    @pl.loop(1, peers)
-    def _(off):
-        pl.semaphore_signal(
-            barrier,
-            inc=1,
-            device_id=place(lax.rem(me + off, peers)),
-            device_id_type=pl.DeviceIdType.MESH,
-        )
+    def signal(_, spot):
+        pl.semaphore_signal(barrier, inc=1, device_id=spot, device_id_type=pl.DeviceIdType.MESH)
+
+    around(signal)
 
 
 def hear(peers):
     pl.semaphore_wait(pltpu.get_barrier_semaphore(), peers - 1)
 
 
-def send(source, target, send_sem, recv_sem, peer):
+def send(source, target, send_sem, recv_sem, spot):
     return pltpu.make_async_remote_copy(
         src_ref=source,
         dst_ref=target,
         send_sem=send_sem,
         recv_sem=recv_sem,
-        device_id=place(peer),
+        device_id=spot,
         device_id_type=pl.DeviceIdType.MESH,
     )
 
 
-def await_all(source, target, send_sem, recv_sem, peers):
-    rest = send(
-        source.at[pl.ds(0, peers - 1)],
-        target.at[pl.ds(0, peers - 1)],
-        send_sem,
-        recv_sem,
-        lax.rem(position() + 1, peers),
-    )
-    rest.wait_send()
-    rest.wait_recv()
+def others(source, target, send_sem, recv_sem, peers):
+    part = pl.ds(0, peers - 1)
+    spot = (lax.axis_index("cx"), lax.axis_index("cy"))
+    return send(source.at[part], target.at[part], send_sem, recv_sem, spot)
 
 
 def invert(idx_ref, inv_ref, acc):
@@ -178,27 +183,26 @@
 ):
     peers = out_ref.shape[0]
     me = position()
-    greet(peers)
+    greet()
     project(params_ref, table, stage)
     hear(peers)
 
-    @pl.loop(1, peers)
-    def _(off):
-        peer = lax.rem(me + off, peers)
-        send(req_ref.at[peer], asked_v.at[me], send1, recv1, peer).start()
-
+    def ask(peer, spot):
+        send(req_ref.at[peer], asked_v.at[me], send1, recv1, spot).start()
+
+    def answer(peer, spot):
+        outgoing[peer] = table[asked_s[peer, 0, 0]]
+        send(outgoing.at[peer], out_ref.at[me], send2, recv2, spot).start()
+
+    around(ask)
     asked_v[me] = req_ref[me]
-    await_all(req_ref, asked_v, send1, recv1, peers)
+    rest = others(req_ref, asked_v, send1, recv1, peers)
+    rest.wait_send()
+    rest.wait_recv()
     copy = pltpu.make_async_copy(asked_v, asked_s, local)
     copy.start()
     copy.wait()
-
-    @pl.loop(1, peers)
-    def _(off):
-        peer = lax.rem(me + off, peers)
-        outgoing[peer] = table[asked_s[peer, 0, 0]]
-        send(outgoing.at[peer], out_ref.at[me], send2, recv2, peer).start()
-
+    around(answer)
     out_ref[me] = table[asked_s[me, 0, 0]]
 
     @pl.loop(0, peers)
@@ -206,7 +210,9 @@
         asked_ref[d] = asked_s[d, 0, 0]
 
     invert(idx_ref, inv_ref, acc)
-    await_all(outgoing, out_ref, send2, recv2, peers)
+    rest = others(outgoing, out_ref, send2, recv2, peers)
+    rest.wait_send()
+    rest.wait_recv()
 
 
 def return_kernel(
@@ -215,13 +221,18 @@
     peers = out_ref.shape[0]
     me = position()
     steps = peers // 8
-    greet(peers)
+    greet()
     fill_table(lambda c: grad_ref[c * LANES : (c + 1) * LANES, :], table, EXACT_BACK)
-    hear(peers)
+    minor = lax.axis_size("cy")
+
+    def send_group(t):
+        for q in range(8):
+            spot = (t * 8 // minor, t * 8 % minor + q)
+            send(outgoing.at[t * 8 + q], out_ref.at[me], send_sem, recv_sem, spot).start()
 
     @pl.loop(1, steps + 1)
     def _(n):
-        t = lax.rem(me // 8 + n, steps)
+        t = wrap(me // 8 + n, steps)
         rows = pick(
             inv_ref[rows8(t), :], table, EXACT_BACK, folded,
             lambda c, h: grad_ref[c * LANES + h : c * LANES + h + 1, :],
@@ -229,29 +240,42 @@
         for c in range(NFEAT):
             outgoing[pl.ds(t * 8, 8), c, :] = rows[c]
 
-        @pl.when(n < steps)
+        @pl.when(n == HEAR)
+        def _():
+            hear(peers)
+
+            @pl.loop(1, HEAR)
+            def _(k):
+                send_group(wrap(me // 8 + k, steps))
+
+        @pl.when((n >= HEAR) & (n < steps))
+        def _():
+            send_group(t)
+
+        major, first = t * 8 // minor, t * 8 % minor
+
+        @pl.when(n == steps)
         def _():
             for q in range(8):
-                peer = t * 8 + q
-                send(outgoing.at[peer], out_ref.at[me], send_sem, recv_sem, peer).start()
-
-    @pl.loop(0, 8)
-    def _(q):
-        peer = me // 8 * 8 + q
-
-        @pl.when(peer != me)
-        def _():
-            send(outgoing.at[peer], out_ref.at[me], send_sem, recv_sem, peer).start()
+
+                @pl.when(t * 8 + q != me)
+                def _():
+                    send(
+                        outgoing.at[t * 8 + q], out_ref.at[me], send_sem, recv_sem,
+                        (major, first + q),
+                    ).start()
 
     out_ref[me] = outgoing[me]
-    await_all(outgoing, out_ref, send_sem, recv_sem, peers)
+    rest = others(outgoing, out_ref, send_sem, recv_sem, peers)
+    rest.wait_send()
+    rest.wait_recv()
 
 
 def unproject_kernel(params_ref, asked_ref, grad_ref, out_ref, stage):
     blocks = grad_ref.shape[0]
     stage_blocks(params_ref, asked_ref, stage, blocks)
 
-    @pl.loop(0, blocks // 8)
+    @pl.loop(0, blocks // 8, unroll=4)
     def _(i):
         par = [stage[pl.ds(i * 128 + c, 8, stride=16), :] for c in range(NPAR)]
         rows = pl.ds(pl.multiple_of(i * 8, 8), 8)
@@ -332,6 +356,7 @@
 
 EXACT = 3
 EXACT_BACK = 3
+HEAR = 6
 PART = 1024
 KC = 16
 NB = 6
@@ -354,7 +379,7 @@
 def render_kernel(
     feat_ref, idx_ref, len_ref, off_ref, cot_ref, spread_ref, reduce_ref,
     img_ref, gsc_ref,
-    table, folded, picked, stack, left, bcast, alpha, weight, trans, image, cots, moms, meta,
+    table, folded, picked, stack, left, bcast, alpha, weight, trans, image, cots, sums, moms, meta,
 ):
     steps = idx_ref.shape[0] // 8
     fill_table(lambda c: feat_ref[:, c, :], table, EXACT)
@@ -392,8 +417,7 @@
         ):
             picked[at_step(c, i), :] = val
 
-    @pl.loop(0, steps)
-    def _(i):
+    def coefficients(i, stack):
         f = [picked[at_step(c, i), :] for c in range(NFEAT)]
         live = (i * KC + lane // TG) < meta[0:8, :]
         u = f[0] - meta[8:16, :].astype(f32)
@@ -422,6 +446,11 @@
         left[pl.ds(pl.multiple_of(i * LANES, LANES), LANES), :] = jnp.concatenate(
             [stack[:LANES].T, stack[LANES:].T], axis=1
         ).astype(bf16)
+
+    @pl.loop(0, steps // 4)
+    def _(j):
+        for q in range(4):
+            coefficients(j * 4 + q, stack.at[q * 256 : (q + 1) * 256])
 
     bcast[...] = jnp.dot(left[...], spread_ref[...], preferred_element_type=f32)
 
@@ -461,35 +490,50 @@
                     image[(c * SIDE + yi[p]) * 8 : (c * SIDE + yi[p]) * 8 + 8, :] = im[c, p]
 
     def backward(i):
-        behind = {y: trans[y * 8 : y * 8 + 8, :] for y in range(SIDE)}
-        for kl in reversed(range(KC)):
-            row = pl.ds(pl.multiple_of(i * (KC * 8) + kl * 8, 8), 8)
-            cols = [bcast[row, n * LANES : (n + 1) * LANES] for n in range(3, NB)]
-            acc = [None] * NB
-
-            def add(n, val):
-                acc[n] = val if acc[n] is None else acc[n] + val
-
-            for n in range(SIDE // 2):
-                dq = {}
-                for sg in (1, -1):
-                    y = 8 + n if sg > 0 else 7 - n
-                    at = pl.ds(pl.multiple_of((i * KC + kl) * PIX // 2 + y * 8, 8), 8)
-                    al, w = alpha[at, :], weight[at, :]
-                    ct = [cots[(c * SIDE + y) * 8 : (c * SIDE + y + 1) * 8, :] for c in range(3)]
-                    d = cols[0] * ct[0] + cols[1] * ct[1] + cols[2] * ct[2] - behind[y]
-                    behind[y] = behind[y] + al * d
-                    dq[sg] = jnp.where(al < 0.99, w * d, 0.0)
-                    for c in range(3):
-                        add(3 + c, w * ct[c])
-                both, diff = dq[1] + dq[-1], dq[1] - dq[-1]
-                add(0, both)
-                add(1, YS[n] * diff)
-                add(2, (YS[n] * YS[n]) * both)
-            for n in range(NB):
-                bcast[row, n * LANES : (n + 1) * LANES] = acc[n]
-        for y in range(SIDE):
-            trans[y * 8 : y * 8 + 8, :] = behind[y]
+        for hb in range(2):
+            ns = range(4 * hb, 4 * hb + 4)
+            ys = [y for n in ns for y in (8 + n, 7 - n)]
+            behind = {y: trans[y * 8 : y * 8 + 8, :] for y in ys}
+            ct = {
+                (c, y): cots[(c * SIDE + y) * 8 : (c * SIDE + y + 1) * 8, :]
+                for y in ys
+                for c in range(3)
+            }
+            for kl in reversed(range(KC)):
+                row = pl.ds(pl.multiple_of(i * (KC * 8) + kl * 8, 8), 8)
+                cols = [bcast[row, n * LANES : (n + 1) * LANES] for n in range(3, NB)]
+                acc = [None] * NB
+
+                def add(n, val):
+                    acc[n] = val if acc[n] is None else acc[n] + val
+
+                for n in ns:
+                    dq = {}
+                    for sg in (1, -1):
+                        y = 8 + n if sg > 0 else 7 - n
+                        at = pl.ds(pl.multiple_of((i * KC + kl) * PIX // 2 + y * 8, 8), 8)
+                        al, w = alpha[at, :], weight[at, :]
+                        d = (
+                            cols[0] * ct[0, y] + cols[1] * ct[1, y] + cols[2] * ct[2, y] - behind[y]
+                        )
+                        behind[y] = behind[y] + al * d
+                        dq[sg] = jnp.where(al < 0.99, w * d, 0.0)
+                        for c in range(3):
+                            add(3 + c, w * ct[c, y])
+                    both, diff = dq[1] + dq[-1], dq[1] - dq[-1]
+                    add(0, both)
+                    add(1, YS[n] * diff)
+                    add(2, (YS[n] * YS[n]) * both)
+                for n in range(NB):
+                    at = n * LANES
+                    if hb == 0:
+                        sums[kl * 8 : kl * 8 + 8, at : at + LANES] = acc[n]
+                    else:
+                        bcast[row, at : at + LANES] = (
+                            sums[kl * 8 : kl * 8 + 8, at : at + LANES] + acc[n]
+                        )
+            for y in ys:
+                trans[y * 8 : y * 8 + 8, :] = behind[y]
 
     @pl.loop(0, steps)
     def _(i):
@@ -635,7 +679,7 @@
             pltpu.VMEM(((NFEAT - EXACT) * LANES // 2, 4 * peers), bf16),
             pltpu.VMEM((NFEAT * 64, LANES), f32),
             pltpu.VMEM((NFEAT * LANES, LANES), f32),
-            pltpu.VMEM((256, LANES), f32),
+            pltpu.VMEM((4 * 256, LANES), f32),
             pltpu.VMEM((length * 8, 256), bf16),
             pltpu.VMEM((length * 8, NB * LANES), f32),
             pltpu.VMEM((length * SIDE * 8, LANES), f32),
@@ -643,6 +687,7 @@
             pltpu.VMEM((SIDE * 8, LANES), f32),
             pltpu.VMEM((3 * SIDE * 8, LANES), f32),
             pltpu.VMEM((3 * SIDE * 8, LANES), f32),
+            pltpu.VMEM((KC * 8, NB * LANES), f32),
             pltpu.VMEM((4 * LANES, LANES), f32),
             pltpu.VMEM((24, LANES), jnp.int32),
         ],

time: 102 us -> 95.9 us (0.940)
  Pallas kernels: 98.3 us -> 92 us
    pallas_call x1, Pallas kernels: 22.5 us -> 18.6 us  [give_back(): pl.pallas_call(return_kernel, out_shape=jax.ShapeDtypeStruct((peers, NFEA...]
    pallas_call x1, Pallas kernels: 41.4 us -> 40.1 us  [per_device(): pl.pallas_call(render_kernel, out_shape=(jax.ShapeDtypeStruct((3, tiles,...]
where the time goes in v4:
time: 95.9 us; the launch traced here: 95.7 us
  Pallas kernels  92 us (96%)
  local copies, waits for them, and re-layouts  2.93 us (3%)
    pallas_call x1, Pallas kernels, per_device(): pl.pallas_call(render_kernel, out_shape=(jax.ShapeDtypeStruct((3, tiles,...  40.1 us
    pallas_call x1, Pallas kernels, fetch(): pl.pallas_call(fetch_kernel, out_shape=(jax.ShapeDtypeStruct((peers, NFEA...  29.6 us
    pallas_call x1, Pallas kernels, give_back(): pl.pallas_call(return_kernel, out_shape=jax.ShapeDtypeStruct((peers, NFEA...  18.6 us
    pallas_call x1, Pallas kernels, per_device(): pl.pallas_call(unproject_kernel, out_shape=jax.ShapeDtypeStruct((NPAR, g_...  3.71 us

profile of v4, /device:TPU:1, one launch (start us, length us, event | category | flops | bytes accessed | tf_op | source)
XLA Modules:
  0.0 95.7 jit_solution(8833928119294970718)
XLA Ops:
  0.6 0.0 copy-start.6
  0.6 0.9 broadcast_in_dim.8.req_ref
  1.5 0.0 copy-done.6
  1.5 0.2 reshape.14
  1.7 0.0 copy-start
  1.7 0.4 copy.11
  2.1 0.5 reshape.15.idx_ref
  2.6 0.3 copy-done
  3.0 0.0 copy-start.1
  3.0 0.0 copy-start.2
  3.0 0.0 copy-start.3
  3.0 29.6 %fetch.1 = (f32[128,9,128]{2,1,0:T(8,128)S(1)}, s32[128]{0:T(128)S(1)}, s32[128,128]{1,0:T(8,128)S(1)}) custom-call(s32[128,1,128]{2,1,0:T(1,128)S(1)} %broadcast_in_dim.8.req_ref, f32[14,16384]{1,0:T(8,128)S(1)} %copy-done, s32[128,128]{1,0:T(8,128)S(1)} %reshape.15.idx_ref), custom_call_target="tpu_custom_call" | custom-call | tf_op jit(solution)/shard_map/fetch/pallas_call | solution.py:621
  32.6 0.0 copy-start.4
  32.6 0.0 copy-start.5
  32.6 0.0 copy-done.1
  32.6 0.0 copy-done.2
  32.6 0.0 copy-done.3
  32.6 0.6 copy-done.4
  33.3 0.0 copy-done.5
  33.3 40.1 %render.1 = (f32[3,64,256]{2,1,0:T(8,128)}, f32[1152,128]{1,0:T(8,128)S(1)}) custom-call(f32[128,9,128]{2,1,0:T(8,128)S(1)} %get-tuple-element.7.feat_ref, s32[128,128]{1,0:T(8,128)S(1)} %reshape.15.idx_ref, s32[64]{0:T(128)S(1)} %copy-done.5, s32[2,64]{1,0:T(2,128)S(1)} %bitcast.8, f32[3,64,256]{2,1,0:T(8,128)S(1)} %bitcast.7, ...), custom_call_target="tpu_custom_call" | custom-call | tf_op jit(solution)/shard_map/render/pallas_call | solution.py:670
  73.3 18.6 %give_back.1.grad_ref = f32[128,9,128]{2,1,0:T(8,128)S(1)} custom-call(f32[1152,128]{1,0:T(8,128)S(1)} %get-tuple-element.10.grad_ref, s32[128,128]{1,0:T(8,128)S(1)} %get-tuple-element.11.inv_ref), custom_call_target="tpu_custom_call" | custom-call | tf_op jit(solution)/shard_map/give_back/pallas_call | solution.py:646
  92.0 3.7 %unproject.1 = f32[14,16384]{1,0:T(8,128)} custom-call(f32[14,16384]{1,0:T(8,128)S(1)} %copy-done, s32[128]{0:T(128)S(1)} %get-tuple-element.9.asked_ref, f32[128,9,128]{2,1,0:T(8,128)S(1)} %give_back.1.grad_ref), custom_call_target="tpu_custom_call" | custom-call | tf_op jit(solution)/shard_map/unproject/pallas_call | solution.py:707
Async XLA Ops:
  0.6 0.9 copy-start.6
  1.7 1.2 %copy-start = (f32[14,16384]{1,0:T(8,128)S(1)}, f32[14,16384]{1,0:T(8,128)}, u32[]{:S(2)}) copy-start(f32[14,16384]{1,0:T(8,128)} %params_ref.3) | copy-start | bytes 2752516
  3.0 29.6 %copy-start.1 = (bf16[256,768]{1,0:T(8,128)(2,1)S(1)}, bf16[256,768]{1,0:T(8,128)(2,1)}, u32[]{:S(2)}) copy-start(bf16[256,768]{1,0:T(8,128)(2,1)} %constant.4.clone.spread_ref) | copy-start | bytes 1179652
  3.0 29.7 %copy-start.2 = (f32[64,3,256]{2,0,1:T(8,128)S(1)}, f32[64,3,256]{2,0,1:T(8,128)}, u32[]{:S(2)}) copy-start(f32[64,3,256]{2,0,1:T(8,128)} %param.13) | copy-start | bytes 589828
  3.0 29.7 %copy-start.3 = (bf16[768,128]{1,0:T(8,128)(2,1)S(1)}, bf16[768,128]{1,0:T(8,128)(2,1)}, u32[]{:S(2)}) copy-start(bf16[768,128]{1,0:T(8,128)(2,1)} %constant.5.clone.reduce_ref) | copy-start | bytes 589828
  32.6 0.7 copy-start.4
  32.6 0.7 copy-start.5

commit v5 on v4

--- a/solution.py
+++ b/solution.py
@@ -66,7 +66,7 @@
 def stage_blocks(params_ref, asked_ref, stage, blocks):
     @pl.loop(0, blocks, unroll=8)
     def _(r):
-        col = pl.multiple_of(asked_ref[r] * LANES, LANES)
+        col = pl.multiple_of(asked_ref[0, r] * LANES, LANES)
         stage[pl.ds(pl.multiple_of(r * 16, 16), NPAR), :] = params_ref[:, pl.ds(col, LANES)]
 
 
@@ -177,13 +177,16 @@
 
 
 def fetch_kernel(
-    req_ref, params_ref, idx_ref,
+    want_ref, params_ref, idx_ref,
     out_ref, asked_ref, inv_ref,
-    asked_v, asked_s, table, stage, outgoing, acc, send1, recv1, send2, recv2, local,
+    req_ref, asked_v, asked_row, asked_s, table, stage, outgoing, acc,
+    send1, recv1, send2, recv2, local,
 ):
     peers = out_ref.shape[0]
     me = position()
     greet()
+    wanted = jnp.broadcast_to(want_ref[...], (peers, peers)).T
+    req_ref[...] = wanted.reshape(peers, 1, peers)
     project(params_ref, table, stage)
     hear(peers)
 
@@ -191,7 +194,7 @@
         send(req_ref.at[peer], asked_v.at[me], send1, recv1, spot).start()
 
     def answer(peer, spot):
-        outgoing[peer] = table[asked_s[peer, 0, 0]]
+        outgoing[peer] = table[asked_s[0, peer]]
         send(outgoing.at[peer], out_ref.at[me], send2, recv2, spot).start()
 
     around(ask)
@@ -199,16 +202,17 @@
     rest = others(req_ref, asked_v, send1, recv1, peers)
     rest.wait_send()
     rest.wait_recv()
-    copy = pltpu.make_async_copy(asked_v, asked_s, local)
+    diagonal = lax.broadcasted_iota(jnp.int32, (peers, LANES), 0) == lax.broadcasted_iota(
+        jnp.int32, (peers, LANES), 1
+    )
+    told = jnp.where(diagonal, asked_v[...].reshape(peers, LANES), 0)
+    asked_row[...] = jnp.sum(told, axis=0, keepdims=True)
+    asked_ref[...] = asked_row[...]
+    copy = pltpu.make_async_copy(asked_row, asked_s, local)
     copy.start()
     copy.wait()
     around(answer)
-    out_ref[me] = table[asked_s[me, 0, 0]]
-
-    @pl.loop(0, peers)
-    def _(d):
-        asked_ref[d] = asked_s[d, 0, 0]
-
+    out_ref[me] = table[asked_s[0, me]]
     invert(idx_ref, inv_ref, acc)
     rest = others(outgoing, out_ref, send2, recv2, peers)
     rest.wait_send()
@@ -290,7 +294,7 @@
 
     @pl.loop(0, blocks, unroll=8)
     def _(r):
-        col = pl.multiple_of(asked_ref[r] * LANES, LANES)
+        col = pl.multiple_of(asked_ref[0, r] * LANES, LANES)
         out_ref[:, pl.ds(col, LANES)] = stage[pl.ds(pl.multiple_of(r * 16, 16), NPAR), :]
 
 
@@ -617,19 +621,20 @@
 
 def fetch(requests, params, idx):
     peers = requests.shape[1]
-    wanted = jnp.broadcast_to(requests.reshape(peers, 1, 1), (peers, 1, LANES))
     return pl.pallas_call(
         fetch_kernel,
         out_shape=(
             jax.ShapeDtypeStruct((peers, NFEAT, LANES), f32),
-            jax.ShapeDtypeStruct((peers,), jnp.int32),
+            jax.ShapeDtypeStruct((1, peers), jnp.int32),
             jax.ShapeDtypeStruct((peers, LANES), jnp.int32),
         ),
         in_specs=[VM, VM, VM],
-        out_specs=(VM, SM, VM),
+        out_specs=(VM, VM, VM),
         scratch_shapes=[
             pltpu.VMEM((peers, 1, LANES), jnp.int32),
-            pltpu.SMEM((peers, 1, LANES), jnp.int32),
+            pltpu.VMEM((peers, 1, LANES), jnp.int32),
+            pltpu.VMEM((1, LANES), jnp.int32),
+            pltpu.SMEM((1, LANES), jnp.int32),
             pltpu.VMEM((peers, NFEAT, LANES), f32),
             pltpu.VMEM((peers * 16, LANES), f32),
             pltpu.VMEM((peers, NFEAT, LANES), f32),
@@ -638,7 +643,7 @@
         + [pltpu.SemaphoreType.DMA] * 5,
         compiler_params=pltpu.CompilerParams(collective_id=0, **REMOTE),
         name="fetch",
-    )(wanted, params, idx)
+    )(requests.reshape(1, peers), params, idx)
 
 
 def give_back(grads, inv):

time: 95.9 us -> 94.1 us (0.981)
  Pallas kernels: 92 us -> 90.3 us
    pallas_call x1, Pallas kernels: 29.6 us -> 28 us  [fetch(): pl.pallas_call(fetch_kernel, out_shape=(jax.ShapeDtypeStruct((peers, NFEA...]
where the time goes in v5:
time: 94.1 us; the launch traced here: 93.9 us
  Pallas kernels  90.3 us (96%)
  local copies, waits for them, and re-layouts  2.88 us (3%)
    pallas_call x1, Pallas kernels, per_device(): pl.pallas_call(render_kernel, out_shape=(jax.ShapeDtypeStruct((3, tiles,...  40.1 us
    pallas_call x1, Pallas kernels, fetch(): pl.pallas_call(fetch_kernel, out_shape=(jax.ShapeDtypeStruct((peers, NFEA...  28 us
    pallas_call x1, Pallas kernels, give_back(): pl.pallas_call(return_kernel, out_shape=jax.ShapeDtypeStruct((peers, NFEA...  18.5 us
    pallas_call x1, Pallas kernels, per_device(): pl.pallas_call(unproject_kernel, out_shape=jax.ShapeDtypeStruct((NPAR, g_...  3.71 us
    reshape x3, local copies, waits for them, and re-layouts, per_device(): lists.reshape(8, TG, steps, KC).transpose(2, 0, 3, 1)  1.92 us

profile of v5, /device:TPU:1, one launch (start us, length us, event | category | flops | bytes accessed | tf_op | source)
XLA Modules:
  0.0 93.9 jit_solution(6379655561375971921)
XLA Ops:
  0.6 1.0 %reshape.14 = s32[8,8,16,16]{3,2,1,0:T(8,128)S(1)} reshape(s32[64,256]{1,0:T(8,128)} %param.10) | data formatting | bytes 131072 | tf_op jit(solution)/shard_map/reshape | solution.py:672
  1.7 0.0 copy-start
  1.7 0.4 copy.11
  2.1 0.0 copy-start.5
  2.1 0.5 reshape.15.idx_ref
  2.6 0.3 copy-done
  2.9 0.0 copy-done.5
  2.9 0.0 copy-start.1
  2.9 0.0 copy-start.2
  2.9 0.0 copy-start.3
  2.9 28.0 %fetch.1 = (f32[128,9,128]{2,1,0:T(8,128)S(1)}, s32[1,128]{1,0:T(1,128)S(1)}, s32[128,128]{1,0:T(8,128)S(1)}) custom-call(s32[1,128]{1,0:T(1,128)S(1)} %bitcast.9, f32[14,16384]{1,0:T(8,128)S(1)} %copy-done, s32[128,128]{1,0:T(8,128)S(1)} %reshape.15.idx_ref), custom_call_target="tpu_custom_call" | custom-call | tf_op jit(solution)/shard_map/fetch/pallas_call | solution.py:624
  30.9 0.0 copy-start.4
  30.9 0.0 copy-start.6
  30.9 0.0 copy-done.1
  31.0 0.0 copy-done.2
  31.0 0.0 copy-done.3
  31.0 0.6 copy-done.4
  31.6 0.0 copy-done.6
  31.6 40.1 %render.1 = (f32[3,64,256]{2,1,0:T(8,128)}, f32[1152,128]{1,0:T(8,128)S(1)}) custom-call(f32[128,9,128]{2,1,0:T(8,128)S(1)} %get-tuple-element.7.feat_ref, s32[128,128]{1,0:T(8,128)S(1)} %reshape.15.idx_ref, s32[64]{0:T(128)S(1)} %copy-done.6, s32[2,64]{1,0:T(2,128)S(1)} %bitcast.8, f32[3,64,256]{2,1,0:T(8,128)S(1)} %bitcast.7, ...), custom_call_target="tpu_custom_call" | custom-call | tf_op jit(solution)/shard_map/render/pallas_call | solution.py:675
  71.7 18.5 %give_back.1.grad_ref = f32[128,9,128]{2,1,0:T(8,128)S(1)} custom-call(f32[1152,128]{1,0:T(8,128)S(1)} %get-tuple-element.10.grad_ref, s32[128,128]{1,0:T(8,128)S(1)} %get-tuple-element.11.inv_ref), custom_call_target="tpu_custom_call" | custom-call | tf_op jit(solution)/shard_map/give_back/pallas_call | solution.py:651
  90.2 3.7 %unproject.1 = f32[14,16384]{1,0:T(8,128)} custom-call(f32[14,16384]{1,0:T(8,128)S(1)} %copy-done, s32[1,128]{1,0:T(1,128)S(1)} %get-tuple-element.9.asked_ref, f32[128,9,128]{2,1,0:T(8,128)S(1)} %give_back.1.grad_ref), custom_call_target="tpu_custom_call" | custom-call | tf_op jit(solution)/shard_map/unproject/pallas_call | solution.py:712
Async XLA Ops:
  1.7 1.2 %copy-start = (f32[14,16384]{1,0:T(8,128)S(1)}, f32[14,16384]{1,0:T(8,128)}, u32[]{:S(2)}) copy-start(f32[14,16384]{1,0:T(8,128)} %params_ref.3) | copy-start | bytes 2752516
  2.1 0.8 copy-start.5
  2.9 28.1 %copy-start.1 = (bf16[256,768]{1,0:T(8,128)(2,1)S(1)}, bf16[256,768]{1,0:T(8,128)(2,1)}, u32[]{:S(2)}) copy-start(bf16[256,768]{1,0:T(8,128)(2,1)} %constant.4.clone.spread_ref) | copy-start | bytes 1179652
  2.9 28.1 %copy-start.2 = (f32[64,3,256]{2,0,1:T(8,128)S(1)}, f32[64,3,256]{2,0,1:T(8,128)}, u32[]{:S(2)}) copy-start(f32[64,3,256]{2,0,1:T(8,128)} %param.13) | copy-start | bytes 589828
  2.9 28.1 %copy-start.3 = (bf16[768,128]{1,0:T(8,128)(2,1)S(1)}, bf16[768,128]{1,0:T(8,128)(2,1)}, u32[]{:S(2)}) copy-start(bf16[768,128]{1,0:T(8,128)(2,1)} %constant.5.clone.reduce_ref) | copy-start | bytes 589828
  30.9 0.7 copy-start.4
  30.9 0.7 copy-start.6

commit v6 on v5

--- a/solution.py
+++ b/solution.py
@@ -176,9 +176,26 @@
     inv_ref[half:, :] = inv[:, LANES:]
 
 
+def tile_rows(len_ref, off_ref, meta):
+    slot = lax.broadcasted_iota(jnp.int32, (1, LANES), 1) % TG
+
+    def per_tile(read):
+        rows = []
+        for g in range(8):
+            row = jnp.full((1, LANES), read(g * TG), jnp.int32)
+            for t in range(1, TG):
+                row = jnp.where(slot == t, read(g * TG + t), row)
+            rows.append(row)
+        return jnp.concatenate(rows, axis=0)
+
+    meta[0:8, :] = per_tile(lambda t: len_ref[t])
+    meta[8:16, :] = per_tile(lambda t: off_ref[0, t]) * SIDE + SIDE // 2
+    meta[16:24, :] = per_tile(lambda t: off_ref[1, t]) * SIDE + SIDE // 2
+
+
 def fetch_kernel(
-    want_ref, params_ref, idx_ref,
-    out_ref, asked_ref, inv_ref,
+    want_ref, params_ref, idx_ref, len_ref, off_ref,
+    out_ref, asked_ref, inv_ref, meta_ref,
     req_ref, asked_v, asked_row, asked_s, table, stage, outgoing, acc,
     send1, recv1, send2, recv2, local,
 ):
@@ -188,6 +205,7 @@
     wanted = jnp.broadcast_to(want_ref[...], (peers, peers)).T
     req_ref[...] = wanted.reshape(peers, 1, peers)
     project(params_ref, table, stage)
+    tile_rows(len_ref, off_ref, meta_ref)
     hear(peers)
 
     def ask(peer, spot):
@@ -381,27 +399,13 @@
 
 
 def render_kernel(
-    feat_ref, idx_ref, len_ref, off_ref, cot_ref, spread_ref, reduce_ref,
+    feat_ref, idx_ref, meta, cot_ref, spread_ref, reduce_ref,
     img_ref, gsc_ref,
-    table, folded, picked, stack, left, bcast, alpha, weight, trans, image, cots, sums, moms, meta,
+    table, folded, picked, stack, left, bcast, alpha, weight, trans, image, cots, sums, moms,
 ):
     steps = idx_ref.shape[0] // 8
     fill_table(lambda c: feat_ref[:, c, :], table, EXACT)
     lane = lax.broadcasted_iota(jnp.int32, (8, LANES), 1)
-    slot = lane % TG
-
-    def per_tile(read):
-        rows = []
-        for g in range(8):
-            row = jnp.full((1, LANES), read(g * TG), jnp.int32)
-            for t in range(1, TG):
-                row = jnp.where(slot[:1] == t, read(g * TG + t), row)
-            rows.append(row)
-        return jnp.concatenate(rows, axis=0)
-
-    meta[0:8, :] = per_tile(lambda t: len_ref[t])
-    meta[8:16, :] = per_tile(lambda t: off_ref[0, t]) * SIDE + SIDE // 2
-    meta[16:24, :] = per_tile(lambda t: off_ref[1, t]) * SIDE + SIDE // 2
     stack[...] = jnp.zeros_like(stack)
     trans[...] = jnp.ones_like(trans)
     image[...] = jnp.zeros_like(image)
@@ -619,7 +623,7 @@
 REMOTE = dict(has_side_effects=True, vmem_limit_bytes=40 * 1024 * 1024)
 
 
-def fetch(requests, params, idx):
+def fetch(requests, params, idx, lengths, offsets):
     peers = requests.shape[1]
     return pl.pallas_call(
         fetch_kernel,
@@ -627,9 +631,10 @@
             jax.ShapeDtypeStruct((peers, NFEAT, LANES), f32),
             jax.ShapeDtypeStruct((1, peers), jnp.int32),
             jax.ShapeDtypeStruct((peers, LANES), jnp.int32),
+            jax.ShapeDtypeStruct((24, LANES), jnp.int32),
         ),
-        in_specs=[VM, VM, VM],
-        out_specs=(VM, VM, VM),
+        in_specs=[VM, VM, VM, SM, SM],
+        out_specs=(VM,) * 4,
         scratch_shapes=[
             pltpu.VMEM((peers, 1, LANES), jnp.int32),
             pltpu.VMEM((peers, 1, LANES), jnp.int32),
@@ -643,7 +648,7 @@
         + [pltpu.SemaphoreType.DMA] * 5,
         compiler_params=pltpu.CompilerParams(collective_id=0, **REMOTE),
         name="fetch",
-    )(requests.reshape(1, peers), params, idx)
+    )(requests.reshape(1, peers), params, idx, lengths, offsets)
 
 
 def give_back(grads, inv):
@@ -670,7 +675,7 @@
     tiles, length = lists.shape
     steps = length // KC
     idx = lists.reshape(8, TG, steps, KC).transpose(2, 0, 3, 1).reshape(steps * 8, LANES)
-    fetched, asked, inv = fetch(requests, params, idx)
+    fetched, asked, inv, meta = fetch(requests, params, idx, list_len, offsets.T)
     spread, reduce = constants()
     image, gfeat = pl.pallas_call(
         render_kernel,
@@ -678,7 +683,7 @@
             jax.ShapeDtypeStruct((3, tiles, PIX), f32),
             jax.ShapeDtypeStruct((NFEAT * LANES, LANES), f32),
         ),
-        in_specs=[VM, VM, SM, SM, VM, VM, VM],
+        in_specs=[VM] * 6,
         out_specs=(VM, VM),
         scratch_shapes=[
             pltpu.VMEM(((NFEAT - EXACT) * LANES // 2, 4 * peers), bf16),
@@ -694,15 +699,13 @@
             pltpu.VMEM((3 * SIDE * 8, LANES), f32),
             pltpu.VMEM((KC * 8, NB * LANES), f32),
             pltpu.VMEM((4 * LANES, LANES), f32),
-            pltpu.VMEM((24, LANES), jnp.int32),
         ],
         compiler_params=LIMIT,
         name="render",
     )(
         fetched,
         idx,
-        list_len,
-        offsets.T,
+        meta,
         cotangent.transpose(1, 0, 2),
         spread,
         reduce,

time: 94.1 us -> 93.4 us (level)
  no operation moved by 1% of the time
where the time goes in v6:
time: 93.4 us; the launch traced here: 93.3 us
  Pallas kernels  90.3 us (97%)
  local copies, waits for them, and re-layouts  2.24 us (2%)
    pallas_call x1, Pallas kernels, per_device(): pl.pallas_call(render_kernel, out_shape=(jax.ShapeDtypeStruct((3, tiles,...  39.4 us
    pallas_call x1, Pallas kernels, fetch(): pl.pallas_call(fetch_kernel, out_shape=(jax.ShapeDtypeStruct((peers, NFEA...  28.6 us
    pallas_call x1, Pallas kernels, give_back(): pl.pallas_call(return_kernel, out_shape=jax.ShapeDtypeStruct((peers, NFEA...  18.5 us
    pallas_call x1, Pallas kernels, per_device(): pl.pallas_call(unproject_kernel, out_shape=jax.ShapeDtypeStruct((NPAR, g_...  3.71 us
    reshape x3, local copies, waits for them, and re-layouts, per_device(): lists.reshape(8, TG, steps, KC).transpose(2, 0, 3, 1)  1.92 us

profile of v6, /device:TPU:1, one launch (start us, length us, event | category | flops | bytes accessed | tf_op | source)
XLA Modules:
  0.0 93.3 jit_solution(13522528914927828808)
XLA Ops:
  0.6 1.0 %reshape.14 = s32[8,8,16,16]{3,2,1,0:T(8,128)S(1)} reshape(s32[64,256]{1,0:T(8,128)} %param.10) | data formatting | bytes 131072 | tf_op jit(solution)/shard_map/reshape | solution.py:677
  1.7 0.0 copy-start
  1.7 0.4 copy.11
  2.1 0.0 copy-start.4
  2.1 0.0 copy-start.5
  2.1 0.0 copy-start.6
  2.1 0.5 reshape.15.idx_ref
  2.6 0.3 copy-done
  2.9 0.0 copy-done.4
  2.9 0.0 copy-done.5
  2.9 0.0 copy-done.6
  2.9 0.0 copy-start.1
  2.9 0.0 copy-start.2
  2.9 0.0 copy-start.3
  2.9 28.6 %fetch.1 = (f32[128,9,128]{2,1,0:T(8,128)S(1)}, s32[1,128]{1,0:T(1,128)S(1)}, s32[128,128]{1,0:T(8,128)S(1)}, s32[24,128]{1,0:T(8,128)S(1)}) custom-call(s32[1,128]{1,0:T(1,128)S(1)} %bitcast.9, f32[14,16384]{1,0:T(8,128)S(1)} %copy-done, s32[128,128]{1,0:T(8,128)S(1)} %reshape.15.idx_ref, s32[64]{0:T(128)S(1)} %copy-done.6, s32[2,64]{1,0:T(2,128)S(1)} %bitcast.8), custom_call_target="tpu_custom_call" | custom-call | tf_op jit(solution)/shard_map/fetch/pallas_call | solution.py:628
  31.5 0.0 copy-done.1
  31.5 0.0 copy-done.2
  31.5 0.0 copy-done.3
  31.5 39.4 %render.1 = (f32[3,64,256]{2,1,0:T(8,128)}, f32[1152,128]{1,0:T(8,128)S(1)}) custom-call(f32[128,9,128]{2,1,0:T(8,128)S(1)} %get-tuple-element.8.feat_ref, s32[128,128]{1,0:T(8,128)S(1)} %reshape.15.idx_ref, s32[24,128]{1,0:T(8,128)S(1)} %get-tuple-element.9.meta, f32[3,64,256]{2,1,0:T(8,128)S(1)} %bitcast.7, bf16[256,768]{1,0:T(8,128)(2,1)S(1)} %copy-done.1, ...), custom_call_target="tpu_custom_call" | custom-call | tf_op jit(solution)/shard_map/render/pallas_call | solution.py:680
  71.0 18.5 %give_back.1.grad_ref = f32[128,9,128]{2,1,0:T(8,128)S(1)} custom-call(f32[1152,128]{1,0:T(8,128)S(1)} %get-tuple-element.12.grad_ref, s32[128,128]{1,0:T(8,128)S(1)} %get-tuple-element.13.inv_ref), custom_call_target="tpu_custom_call" | custom-call | tf_op jit(solution)/shard_map/give_back/pallas_call | solution.py:656
  89.5 3.7 %unproject.1 = f32[14,16384]{1,0:T(8,128)} custom-call(f32[14,16384]{1,0:T(8,128)S(1)} %copy-done, s32[1,128]{1,0:T(1,128)S(1)} %get-tuple-element.11.asked_ref, f32[128,9,128]{2,1,0:T(8,128)S(1)} %give_back.1.grad_ref), custom_call_target="tpu_custom_call" | custom-call | tf_op jit(solution)/shard_map/unproject/pallas_call | solution.py:715
Async XLA Ops:
  1.7 1.2 %copy-start = (f32[14,16384]{1,0:T(8,128)S(1)}, f32[14,16384]{1,0:T(8,128)}, u32[]{:S(2)}) copy-start(f32[14,16384]{1,0:T(8,128)} %params_ref.3) | copy-start | bytes 2752516
  2.1 0.8 copy-start.4
  2.1 0.8 copy-start.5
  2.1 0.8 copy-start.6
  2.9 28.6 %copy-start.1 = (bf16[256,768]{1,0:T(8,128)(2,1)S(1)}, bf16[256,768]{1,0:T(8,128)(2,1)}, u32[]{:S(2)}) copy-start(bf16[256,768]{1,0:T(8,128)(2,1)} %constant.4.clone.spread_ref) | copy-start | bytes 1179652
  2.9 28.6 %copy-start.2 = (f32[64,3,256]{2,0,1:T(8,128)S(1)}, f32[64,3,256]{2,0,1:T(8,128)}, u32[]{:S(2)}) copy-start(f32[64,3,256]{2,0,1:T(8,128)} %param.13) | copy-start | bytes 589828
  2.9 28.6 %copy-start.3 = (bf16[768,128]{1,0:T(8,128)(2,1)S(1)}, bf16[768,128]{1,0:T(8,128)(2,1)}, u32[]{:S(2)}) copy-start(bf16[768,128]{1,0:T(8,128)(2,1)} %constant.5.clone.reduce_ref) | copy-start | bytes 589828
